TPU v7x, 32 devices: a whole 2x2x4 slice. The times are simulated.
32 devices in a mesh: panel: 4 (over y, x), front: 8 (over z, core).
Axes of the slice: x: 2, y: 2, z: 4, core: 2. Of those that a mesh axis runs over, the one named last changes fastest.
Arguments:
- leaf_inv: float32 [4, 8, 768, 768], P('panel', 'front'), may hold values from -0.21875 to 0.21875
- parent_inv: float32 [4, 8, 768, 768], P('panel', 'front'), may hold values from -0.21875 to 0.21875
- up_coupling: float32 [4, 8, 384, 768], P('panel', 'front'), may hold values from -0.21875 to 0.21875
- down_coupling: float32 [4, 8, 768, 384], P('panel', 'front'), may hold values from -0.3125 to 0.3125
- interface_coupling: float32 [4, 8, 768, 512], P('panel', 'front'), may hold values from -0.25 to 0.25
- leaf_sources: float32 [4, 8, 3, 768, 128], P('panel', 'front'), may hold values from -6 to 6
- parent_sources: float32 [4, 8, 3, 768, 128], P('panel', 'front'), may hold values from -6 to 6
- parent_of: int32 [4, 8], P('panel'), may hold values from 0 to 7
- update_count: int32 [4, 8], P('panel'), may hold values from 128 to 384, as said below
- update_rows: int32 [4, 8, 384], P('panel'), may hold values from 0 to 767, as said below
Outputs:
- leaf_solution: float32 [4, 8, 3, 768, 128], P('panel', 'front')
- parent_solution: float32 [4, 8, 3, 768, 128], P('panel', 'front')
Inputs may be any that keep to these rules, and one draw needn't show every extreme that they name: `update_count`: a multiple of 128; some leaf of every panel has 384. `update_rows`: the entries of one leaf are distinct; those at or past its update_count are padding.
All inputs are finite; a program needn't handle non-finite values.
Results may differ from a plain program's by a relative error of at most 0.0003.
Values sent between devices are 32-bit elements; how exact they have to be, the bound alone decides.
No kernel may reach another device: no remote copies, remote signals or barrier semaphores. Data moves between devices by JAX's collectives and lax.ppermute only.
A program may use at most 128 MiB of HBM per device.

v0:
```python
import jax
import jax.numpy as jnp
from jax import lax
from jax.sharding import PartitionSpec as P

TICKS = 3


highest_precision = lax.Precision.HIGHEST


def passed_along(value, axis, steps):
    count = lax.axis_size(axis)
    leading, last = (max(0, -steps), min(count, count - steps))
    return lax.ppermute(value, axis, [(source, source + steps) for source in range(leading, last)])


def product(matrix, operand):
    return jnp.dot(matrix, operand, precision=highest_precision, preferred_element_type=jnp.float32)


def local(
    leaf_inv,
    parent_inv,
    up_coupling,
    down_coupling,
    interface_coupling,
    leaf_sources,
    parent_sources,
    parent_of,
    update_count,
    update_rows,
):
    inverse = leaf_inv[0, 0]
    parent_inverse = parent_inv[0, 0]
    upward = up_coupling[0, 0]
    downward = down_coupling[0, 0]
    coupling = interface_coupling[0, 0]
    leaf_order = inverse.shape[0]
    parent_order = parent_inverse.shape[0]
    iface_rows = coupling.shape[1]
    parents = parent_of[0]
    counts = update_count[0]
    row_ids = update_rows[0]
    update_cap = row_ids.shape[1]
    myself = lax.axis_index("front")
    slot_ids = jnp.arange(update_cap, dtype=jnp.int32)[None, :]
    live_slots = slot_ids < counts[:, None]
    mine = live_slots & (parents[:, None] == myself)
    targets = jnp.where(mine, row_ids, parent_order).reshape(-1)
    own_live = lax.dynamic_index_in_dim(live_slots, myself, 0, keepdims=False)
    own_rows = lax.dynamic_index_in_dim(row_ids, myself, 0, keepdims=False)
    own_parent = lax.dynamic_index_in_dim(parents, myself, 0, keepdims=False)
    leaf_list = []
    parent_list = []
    previous = None
    for tick_index in range(TICKS):
        sources = leaf_sources[0, 0, tick_index]
        interface = None
        if tick_index > 0:
            interface = passed_along(previous[leaf_order - iface_rows :], "panel", 1)
        partial_solution = product(inverse, sources)
        if interface is not None:
            partial_solution = partial_solution + product(inverse, product(coupling, interface))
        update = jnp.where(own_live[:, None], product(upward, partial_solution), 0.0)
        everyone = lax.all_gather(update, "front", axis=0, tiled=True)
        assembled = jax.ops.segment_sum(everyone, targets, num_segments=parent_order + 1)[
            :parent_order
        ]
        solved = product(parent_inverse, parent_sources[0, 0, tick_index] - assembled)
        all_parents = lax.all_gather(solved, "front", axis=0, tiled=True)
        take_index = own_parent * parent_order + own_rows
        picked = jnp.where(own_live[:, None], jnp.take(all_parents, take_index, axis=0), 0.0)
        leaf_now = partial_solution - product(downward, picked)
        leaf_list.append(leaf_now)
        parent_list.append(solved)
        previous = leaf_now
    leaf_out = jnp.stack(leaf_list, axis=0)[None, None]
    parent_out = jnp.stack(parent_list, axis=0)[None, None]
    return (leaf_out, parent_out)


def solution(mesh):
    placed = (
        P("panel", "front", None, None),
        P("panel", "front", None, None),
        P("panel", "front", None, None),
        P("panel", "front", None, None),
        P("panel", "front", None, None),
        P("panel", "front", None, None, None),
        P("panel", "front", None, None, None),
        P("panel", None),
        P("panel", None),
        P("panel", None, None),
    )
    return jax.shard_map(
        local,
        mesh=mesh,
        in_specs=placed,
        out_specs=(P("panel", "front", None, None, None), P("panel", "front", None, None, None)),
        check_vma=False,
    )
```

profile of v0, /device:TPU:0, one launch (start us, length us, event | category | flops | bytes accessed | tf_op | source)
XLA Modules:
  0.0 358.1 jit_solution(15863737149855156628)
XLA Ops:
  8.9 3.1 fusion.14
  15.9 26.5 %all-gather.7.cloned.1.call-done = f32[3072,128]{1,0:T(8,128)} async-done(((f32[384,128]{1,0:T(8,128)}), f32[3072,128]{1,0:T(8,128)}) %all-gather.7.cloned.1.call-update) | async-done | bytes 1572880 | tf_op jit(solution)/shard_map/all_gather | solution.py:66
  42.4 22.8 %scatter_custom_fusion = f32[769,128]{1,0:T(8,128)} fusion(s32[3072]{0:T(1024)} %bitcast.157, f32[3072,128]{1,0:T(8,128)} %all-gather.7.cloned.1.call-done, f32[]{:T(128)} %constant.34.clone.1), kind=kCustom, calls=%fused_computation.73 | custom fusion | flops 393216 | bytes 394240 | tf_op jit(solution)/shard_map/scatter-add | solution.py:67
  65.2 4.8 %fusion.4 = f32[128,768]{1,0:T(8,128)} fusion(f32[1,1,768,768]{3,2,1,0:T(8,128)} %param.13, f32[769,128]{1,0:T(8,128)} %scatter_custom_fusion, f32[1,1,3,768,128]{4,3,2,1,0:T(8,128)} %param.18), kind=kOutput, calls=%fused_computation.10 | convolution fusion | flops 906067968 | bytes 3538944 | tf_op jit(solution)/shard_map/dot_general | solution.py:19
  72.1 35.8 %all-gather.9.cloned.1.call-done = f32[6144,128]{0,1:T(8,128)} async-done(((f32[768,128]{0,1:T(8,128)}), f32[6144,128]{0,1:T(8,128)}) %all-gather.9.cloned.1.call-update) | async-done | bytes 3145744 | tf_op jit(solution)/shard_map/all_gather | solution.py:71
  107.9 3.6 copy.12
  111.5 3.5 gather_fusion
  118.4 3.7 %collective-permute-start = (f32[512,128]{1,0:T(8,128)S(1)}, f32[512,128]{1,0:T(8,128)S(1)}, u32[]{:S(2)}, u32[]{:S(2)}) collective-permute-start(f32[512,128]{1,0:T(8,128)S(1)} %slice.51), channel_id=1, source_target_pairs={{0,8},{8,16},{16,24},{1,9},{9,17},{17,25},{2,10},{10,18},{18,26},{... | collective-permute-start | bytes 786440 | tf_op jit(solution)/shard_map/ppermute | solution.py:15
  122.1 3.0 fusion.12
  134.0 25.0 %all-gather.11.cloned.1.call-done = f32[3072,128]{1,0:T(8,128)} async-done(((f32[384,128]{1,0:T(8,128)}), f32[3072,128]{1,0:T(8,128)}) %all-gather.11.cloned.1.call-update) | async-done | bytes 1572880 | tf_op jit(solution)/shard_map/all_gather | solution.py:66
  159.0 22.8 %scatter_custom_fusion.1 = f32[769,128]{1,0:T(8,128)} fusion(s32[3072]{0:T(1024)} %bitcast.158, f32[3072,128]{1,0:T(8,128)} %all-gather.11.cloned.1.call-done, f32[]{:T(128)} %constant.34.clone.1), kind=kCustom, calls=%fused_computation.71 | custom fusion | flops 393216 | bytes 394240 | tf_op jit(solution)/shard_map/scatter-add | solution.py:67
  181.8 4.8 %fusion.2 = f32[128,768]{1,0:T(8,128)} fusion(f32[1,1,768,768]{3,2,1,0:T(8,128)} %param.13, f32[769,128]{1,0:T(8,128)} %scatter_custom_fusion.1, f32[1,1,3,768,128]{4,3,2,1,0:T(8,128)} %param.18), kind=kOutput, calls=%fused_computation.8 | convolution fusion | flops 906067968 | bytes 3538944 | tf_op jit(solution)/shard_map/dot_general | solution.py:19
  186.9 37.6 %all-gather.13.cloned.1.call-done = f32[6144,128]{0,1:T(8,128)} async-done(((f32[768,128]{0,1:T(8,128)}), f32[6144,128]{0,1:T(8,128)}) %all-gather.13.cloned.1.call-update) | async-done | bytes 3145744 | tf_op jit(solution)/shard_map/all_gather | solution.py:71
  224.5 3.6 copy.15
  228.0 3.5 gather_fusion.1
  235.0 3.5 collective-permute-start.1
  238.5 3.0 fusion.8
  241.5 2.9 collective-permute-done.1
  250.5 25.0 %all-gather.15.cloned.1.call-done = f32[3072,128]{1,0:T(8,128)} async-done(((f32[384,128]{1,0:T(8,128)}), f32[3072,128]{1,0:T(8,128)}) %all-gather.15.cloned.1.call-update) | async-done | bytes 1572880 | tf_op jit(solution)/shard_map/all_gather | solution.py:66
  275.5 22.4 %scatter_custom_fusion.2 = f32[769,128]{1,0:T(8,128)S(1)} fusion(s32[3072]{0:T(1024)} %bitcast.159, f32[3072,128]{1,0:T(8,128)} %all-gather.15.cloned.1.call-done, f32[]{:T(128)} %constant.34.clone.1), kind=kCustom, calls=%fused_computation.69 | custom fusion | flops 393216 | bytes 394240 | tf_op jit(solution)/shard_map/scatter-add | solution.py:67
  297.9 4.7 %fusion = f32[128,768]{1,0:T(8,128)} fusion(f32[1,1,768,768]{3,2,1,0:T(8,128)} %param.13, f32[769,128]{1,0:T(8,128)S(1)} %scatter_custom_fusion.2, f32[1,1,3,768,128]{4,3,2,1,0:T(8,128)} %param.18), kind=kOutput, calls=%fused_computation.6 | convolution fusion | flops 906067968 | bytes 3538944 | tf_op jit(solution)/shard_map/dot_general | solution.py:19
  305.4 35.2 %all-gather.17.cloned.1.call-done = f32[6144,128]{0,1:T(8,128)} async-done(((f32[768,128]{0,1:T(8,128)}), f32[6144,128]{0,1:T(8,128)}) %all-gather.17.cloned.1.call-update) | async-done | bytes 3145744 | tf_op jit(solution)/shard_map/all_gather | solution.py:71
  340.5 3.6 copy.18
  344.1 3.6 %gather_fusion.2 = f32[384,128]{1,0:T(8,128)} fusion(f32[6144,128]{1,0:T(8,128)} %copy.18, s32[1024]{0:T(1024)S(1)} %pad_clamp_fusion), kind=kCustom, calls=%fused_computation.2.clone | custom fusion | bytes 394752 | tf_op jit(solution)/shard_map/jit(_take)/gather | solution.py:73
  (65 shorter events, 35.7 us)
Async XLA Ops:
  7.2 1.7 copy-start
  7.2 35.2 %all-gather.7.cloned.1.call-start = ((), (), s32[]{:S(2)}) async-start(), calls=%async_computation | async-start | bytes 1769472 | tf_op jit(solution)/shard_map/all_gather | solution.py:66
  8.9 3.8 %copy-start.1 = (f32[1,1,384,768]{3,2,1,0:T(8,128)S(1)}, f32[1,1,384,768]{3,2,1,0:T(8,128)}, u32[]{:S(2)}) copy-start(f32[1,1,384,768]{3,2,1,0:T(8,128)} %param.14) | copy-start | bytes 3538948
  11.9 0.7 copy-start.5
  14.5 93.4 %all-gather.9.cloned.1.call-start = ((), (), s32[]{:S(2)}) async-start(), calls=%async_computation.1 | async-start | bytes 3538944 | tf_op jit(solution)/shard_map/all_gather | solution.py:71
  65.2 4.9 %copy-start.12 = (s32[1,8]{1,0:T(1,128)S(1)}, s32[1,8]{1,0:T(1,128)}, u32[]{:S(2)}) copy-start(s32[1,8]{1,0:T(1,128)} %param.19) | copy-start | bytes 100
  70.1 88.9 %all-gather.11.cloned.1.call-start = ((), (), s32[]{:S(2)}) async-start(), calls=%async_computation.2 | async-start | bytes 1769472 | tf_op jit(solution)/shard_map/all_gather | solution.py:66
  117.6 0.8 copy-start.8
  118.4 9.5 %copy-start.3 = (f32[1,1,768,512]{3,2,1,0:T(8,128)S(1)}, f32[1,1,768,512]{3,2,1,0:T(8,128)}, u32[]{:S(2)}) copy-start(f32[1,1,768,512]{3,2,1,0:T(8,128)} %param.16) | copy-start | bytes 4718596
  118.4 9.5 %collective-permute-start = (f32[512,128]{1,0:T(8,128)S(1)}, f32[512,128]{1,0:T(8,128)S(1)}, u32[]{:S(2)}, u32[]{:S(2)}) collective-permute-start(f32[512,128]{1,0:T(8,128)S(1)} %slice.51), channel_id=1, source_target_pairs={{0,8},{8,16},{16,24},{1,9},{9,17},{17,25},{2,10},{10,18},{18,26},{... | collective-permute-start | bytes 786440 | tf_op jit(solution)/shard_map/ppermute | solution.py:15
  131.4 0.7 copy-start.7
  133.9 90.6 %all-gather.13.cloned.1.call-start = ((), (), s32[]{:S(2)}) async-start(), calls=%async_computation.3 | async-start | bytes 3538944 | tf_op jit(solution)/shard_map/all_gather | solution.py:71
  186.6 88.9 %all-gather.15.cloned.1.call-start = ((), (), s32[]{:S(2)}) async-start(), calls=%async_computation.4 | async-start | bytes 1769472 | tf_op jit(solution)/shard_map/all_gather | solution.py:66
  234.2 0.7 copy-start.10
  235.0 9.5 %copy-start.4 = (f32[1,1,768,512]{3,2,1,0:T(8,128)S(1)}, f32[1,1,768,512]{3,2,1,0:T(8,128)}, u32[]{:S(2)}) copy-start(f32[1,1,768,512]{3,2,1,0:T(8,128)} %param.16) | copy-start | bytes 4718596
  235.0 9.5 %collective-permute-start.1 = (f32[512,128]{1,0:T(8,128)S(1)}, f32[512,128]{1,0:T(8,128)S(1)}, u32[]{:S(2)}, u32[]{:S(2)}) collective-permute-start(f32[512,128]{1,0:T(8,128)S(1)} %slice.53), channel_id=1, source_target_pairs={{0,8},{8,16},{16,24},{1,9},{9,17},{17,25},{2,10},{10,18},{18,26},{... | collective-permute-start | bytes 786440 | tf_op jit(solution)/shard_map/ppermute | solution.py:15
  247.9 0.7 copy-start.6
  250.4 90.1 %all-gather.17.cloned.1.call-start = ((), (), s32[]{:S(2)}) async-start(), calls=%async_computation.5 | async-start | bytes 3538944 | tf_op jit(solution)/shard_map/all_gather | solution.py:71
  344.1 3.6 %copy-start.2 = (f32[1,1,768,384]{3,2,1,0:T(8,128)S(1)}, f32[1,1,768,384]{3,2,1,0:T(8,128)}, u32[]{:S(2)}) copy-start(f32[1,1,768,384]{3,2,1,0:T(8,128)} %param.15) | copy-start | bytes 3538948
  347.7 2.4 copy-start.9
  347.7 2.4 copy-start.11
Sparse Core Ops, SparseCore 0:
  14.6 27.7 all-gather.6
  70.2 37.6 all-gather.8
  134.0 24.9 all-gather.10
  186.7 37.6 all-gather.12
  250.6 24.9 all-gather.14
  302.8 37.6 all-gather.16
where the time goes:
time: 358 us
  waiting for transfers between devices  191 us (53%)
  other arithmetic  74.6 us (21%)
  matrix products  43.2 us (12%)
  local copies, waits for them, and re-layouts  27.3 us (8%)
  between operations  14.3 us (4%)
  starting transfers between devices  7.69 us (2%)
    all_gather x3, waiting for transfers between devices, local(): all_parents = lax.all_gather(solved, 'front', axis=0, tiled=True)  109 us
    all_gather x3, waiting for transfers between devices, local(): everyone = lax.all_gather(update, 'front', axis=0, tiled=True)  76.6 us
    scatter-add x3, other arithmetic, local(): jax.ops.segment_sum(everyone, targets, num_segments=parent_order + 1)  68.1 us
    dot_general x16, matrix products, product(): jnp.dot(matrix, operand, precision=highest_precision, preferred_element_t...  43.2 us
    all_gather x3, local copies, waits for them, and re-layouts, local(): all_parents = lax.all_gather(solved, 'front', axis=0, tiled=True)  10.7 us
    gather x3, local copies, waits for them, and re-layouts, local(): jnp.take(all_parents, take_index, axis=0)  10.6 us
    ppermute x2, starting transfers between devices, passed_along(): lax.ppermute(value, axis, [(source, source + steps) for source in range(l...  7.23 us
  transfers between devices with their start and end apart: 8, of which 8 were waited for; matrix products, arithmetic and copies ran while one was open for 3% of the time, Pallas kernels for 0%

commit v1 on v0

v1 whole, which is shorter than its diff:
```python
import functools

import jax
import jax.numpy as jnp
from jax import lax
from jax.experimental import pallas as pl
from jax.experimental.pallas import tpu as pltpu
from jax.sharding import PartitionSpec as P

TWIN = 1
VMEM_BYTES = 48 * 1024 * 1024


def swapped(value, mask):
    count = lax.axis_size("front")
    return lax.ppermute(value, "front", [(place, place ^ mask) for place in range(count)])


def onward(value, panel_step, mask):
    panels = lax.axis_size("panel")
    fronts = lax.axis_size("front")
    pairs = []
    for panel in range(panels):
        for place in range(fronts):
            goal = (panel + panel_step) % panels
            pairs.append((panel * fronts + place, goal * fronts + (place ^ mask)))
    return lax.ppermute(value, ("panel", "front"), pairs)


def cube_masks(count):
    masks = []
    low = 2
    while low < count:
        masks.append(2 * low - 2)
        low *= 2
    return masks[::-1]


def offsets(masks):
    held = [0]
    for mask in masks:
        held = held + [offset ^ mask for offset in held]
    return held


def spread(held, masks):
    held = dict(held)
    for mask in masks:
        held.update({offset ^ mask: swapped(value, mask) for offset, value in list(held.items())})
    return held


def delivered(parts, masks):
    parts = dict(parts)
    span = offsets(masks)
    first = None
    for step in range(len(masks) - 1, -1, -1):
        mask = masks[step]
        for offset in span[2 ** step - 1 :: -1]:
            received = swapped(parts.pop(offset ^ mask), mask)
            first = received if first is None else first
            parts[offset] = parts[offset] + received
    return parts[0], first


def product(matrix, operand):
    return jnp.dot(matrix, operand, precision=lax.Precision.HIGH, preferred_element_type=jnp.float32)


def prepared(matrix, operand):
    return jnp.dot(matrix, operand, precision=lax.Precision.HIGHEST, preferred_element_type=jnp.float32)


def halves(value):
    rounded = lax.reduce_precision(value, 8, 7)
    return rounded.astype(jnp.bfloat16), (value - rounded).astype(jnp.bfloat16)


def side_by_side(value):
    high = value.astype(jnp.bfloat16)
    low = (value - high.astype(jnp.float32)).astype(jnp.bfloat16)
    return jnp.concatenate([high, low], axis=1)


def summed(pair):
    columns = pair.shape[1] // 2
    return pair[:, :columns] + pair[:, columns:]


def after(value, event):
    return lax.optimization_barrier((value, event))[0]


def solve_kernel(offsets_in, place, parents, rows, high, low, sources, *refs):
    blocks, out, rhs = refs[:-2], refs[-2], refs[-1]
    rhs[...] = sources[...]
    extent = (rhs.shape[0], rows.shape[1])
    for offset, block in zip(offsets_in, blocks):
        leaf = place[0] ^ offset

        @pl.when(parents[0, leaf] == place[0])
        def _():
            choice = lax.broadcasted_iota(jnp.int32, extent, 0) == rows[pl.ds(leaf, 1), :]
            pair = jnp.dot(
                jnp.where(choice, 1.0, 0.0).astype(jnp.bfloat16),
                side_by_side(block[...]),
                preferred_element_type=jnp.float32,
            )
            rhs[...] -= summed(pair)

    both = side_by_side(rhs[...])
    columns = out.shape[1]
    out[...] = summed(jnp.dot(high[...], both, preferred_element_type=jnp.float32)) + jnp.dot(
        low[...], both[:, :columns], preferred_element_type=jnp.float32
    )


def parent_solve(place, parents, rows, high, low, sources, blocks):
    order = sources.shape[0]
    depth = sum(block.shape[0] for block in blocks.values())
    smem = pl.BlockSpec(memory_space=pltpu.SMEM)
    vmem = pl.BlockSpec(memory_space=pltpu.VMEM)
    return pl.pallas_call(
        functools.partial(solve_kernel, list(blocks)),
        out_shape=jax.ShapeDtypeStruct(sources.shape, jnp.float32),
        in_specs=[smem] * 2 + [vmem] * (4 + len(blocks)),
        out_specs=vmem,
        scratch_shapes=[pltpu.VMEM(sources.shape, jnp.float32)],
        compiler_params=pltpu.CompilerParams(vmem_limit_bytes=VMEM_BYTES),
        cost_estimate=pl.CostEstimate(
            flops=8 * order * order * sources.shape[1],
            bytes_accessed=4 * order * (order + 256) + 512 * depth,
            transcendentals=0,
        ),
        name="parent_solve",
    )(place, parents, rows, high, low, sources, *blocks.values())


def rows_kernel(offsets_out, place, parents, counts, rows, own, other, *refs):
    outs, wide = refs[:-1], refs[-1]
    wide[0] = side_by_side(own[...])
    wide[1] = side_by_side(other[...])
    cap = rows.shape[1]
    order = own.shape[0]
    lanes = 128
    for offset, out in zip(offsets_out, outs):
        leaf = place[0] ^ offset
        parent = parents[0, leaf]
        mine = parent == place[0]
        here = mine | (parent == (place[0] ^ TWIN))

        @pl.when(jnp.logical_not(here))
        def _():
            out[...] = jnp.zeros_like(out)

        @pl.when(here)
        def _():
            slot = lax.broadcasted_iota(jnp.int32, (lanes, cap), 1)
            column = jnp.where(slot < counts[0, leaf], jnp.broadcast_to(rows[pl.ds(leaf, 1), :], (lanes, cap)), -1).T
            lane = lax.broadcasted_iota(jnp.int32, (cap, lanes), 1)
            choice = jnp.concatenate(
                [jnp.where(column == lane + start, 1.0, 0.0).astype(jnp.bfloat16) for start in range(0, order, lanes)],
                axis=1,
            )
            out[...] = summed(
                jnp.dot(choice, wide[jnp.where(mine, 0, 1)], preferred_element_type=jnp.float32)
            )


def parent_rows(place, parents, counts, rows, own, other, wanted):
    cap = rows.shape[1]
    order, columns = own.shape
    smem = pl.BlockSpec(memory_space=pltpu.SMEM)
    vmem = pl.BlockSpec(memory_space=pltpu.VMEM)
    found = pl.pallas_call(
        functools.partial(rows_kernel, wanted),
        out_shape=[jax.ShapeDtypeStruct((cap, columns), jnp.float32)] * len(wanted),
        in_specs=[smem] * 3 + [vmem] * 3,
        out_specs=[vmem] * len(wanted),
        scratch_shapes=[pltpu.VMEM((2, order, 2 * columns), jnp.bfloat16)],
        compiler_params=pltpu.CompilerParams(vmem_limit_bytes=VMEM_BYTES),
        cost_estimate=pl.CostEstimate(
            flops=4 * cap * order * columns * len(wanted), bytes_accessed=8 * order * columns, transcendentals=0
        ),
        name="parent_rows",
    )(place, parents, counts, rows, own, other)
    return dict(zip(wanted, found))


def local(
    leaf_inv,
    parent_inv,
    up_coupling,
    down_coupling,
    interface_coupling,
    leaf_sources,
    parent_sources,
    parent_of,
    update_count,
    update_rows,
):
    inverse = leaf_inv[0, 0]
    upward = up_coupling[0, 0]
    downward = down_coupling[0, 0]
    coupling = interface_coupling[0, 0]
    ticks = leaf_sources.shape[2]
    columns = leaf_sources.shape[4]
    leaf_order = inverse.shape[0]
    iface_rows = coupling.shape[1]
    row_ids = update_rows[0]
    fronts = lax.axis_size("front")
    panels = lax.axis_size("panel")
    myself = lax.axis_index("front")
    place = myself.astype(jnp.int32).reshape(1)
    masks = cube_masks(fronts)
    span = offsets(masks)
    own_count = lax.dynamic_index_in_dim(update_count[0], myself, 0, keepdims=False)
    own_live = (jnp.arange(row_ids.shape[1], dtype=jnp.int32) < own_count)[:, None]

    def edge(value):
        return value[leaf_order - iface_rows :]

    sources = leaf_sources[0, 0]
    partial_solution = product(inverse, sources[0])
    update = jnp.where(own_live, product(upward, partial_solution), 0.0)
    held = spread({0: update}, masks)
    parent_high, parent_low = halves(parent_inv[0, 0])

    later = jnp.concatenate([sources[tick] for tick in range(1, ticks)], axis=1)
    along = jnp.where(own_live, prepared(upward, inverse), 0.0)
    through = jnp.where(lax.axis_index("panel") > 0, prepared(along, coupling), 0.0)
    next_through = onward(through, -1, 0)
    next_sources = onward(product(along, later), -1, 0)
    next_descended = prepared(next_through, edge(downward))
    own_later = product(inverse, later)

    leaf_list = []
    parent_list = []
    interface = None
    for tick in range(ticks):
        blocks = {offset: held[offset] for offset in span}
        blocks.update({offset ^ TWIN: swapped(held[offset], TWIN) for offset in span})
        solved = parent_solve(
            place, parent_of, row_ids, parent_high, parent_low, parent_sources[0, 0, tick], blocks
        )
        parent_list.append(solved)
        parts = parent_rows(place, parent_of, update_count, row_ids, solved, swapped(solved, TWIN), span)
        descended, first = delivered(parts, masks)
        at = slice((tick - 1) * columns, tick * columns)
        if tick > 0:
            arrived = after(interface, first)
            partial_solution = own_later[:, at] + product(inverse, product(coupling, arrived))
        if tick + 1 < ticks:
            at = slice(tick * columns, (tick + 1) * columns)
            base = next_sources[:, at] + product(next_through, edge(partial_solution))
            update = base - product(next_descended, descended)
            moved = onward(update, 1, 0)
            held = spread({0: moved, masks[0]: onward(update, 1, masks[0])}, masks[1:])
            leaf_now = partial_solution - product(downward, after(descended, moved))
            interface = lax.ppermute(edge(leaf_now), "panel", [(spot, spot + 1) for spot in range(panels - 1)])
        else:
            leaf_now = partial_solution - product(downward, descended)
        leaf_list.append(leaf_now)
    leaf_out = jnp.stack(leaf_list, axis=0)[None, None]
    parent_out = jnp.stack(parent_list, axis=0)[None, None]
    return (leaf_out, parent_out)


def solution(mesh):
    placed = (
        P("panel", "front", None, None),
        P("panel", "front", None, None),
        P("panel", "front", None, None),
        P("panel", "front", None, None),
        P("panel", "front", None, None),
        P("panel", "front", None, None, None),
        P("panel", "front", None, None, None),
        P("panel", None),
        P("panel", None),
        P("panel", None, None),
    )
    return jax.shard_map(
        local,
        mesh=mesh,
        in_specs=placed,
        out_specs=(P("panel", "front", None, None, None), P("panel", "front", None, None, None)),
        check_vma=False,
    )
```

time: 358 us -> 153 us (0.43)
  waiting for transfers between devices: 191 us -> 69.6 us
  other arithmetic: 74.6 us -> 3.34 us
  starting transfers between devices: 7.69 us -> 45.7 us
  local copies, waits for them, and re-layouts: 27.3 us -> 2.63 us
  matrix products: 43.2 us -> 22.9 us
  between operations: 14.3 us -> 1.1 us
  Pallas kernels: 0 us -> 10.6 us
    all_gather x6 -> x0, waiting for transfers between devices: 185 us -> none  [the longest x3 109 us: local(): all_parents = lax.all_gather(solved, 'front', axis=0, tiled=True)]
    scatter-add x3 -> x0, other arithmetic: 68.1 us -> none  [local(): jax.ops.segment_sum(everyone, targets, num_segments=parent_order + 1)]
    ppermute x2 -> x39, waiting for transfers between devices: 5.68 us -> 69.6 us  [the longest x31 48.1 us: swapped(): lax.ppermute(value, 'front', [(place, place ^ mask) for place in range(co...]
    ppermute x2 -> x39, starting transfers between devices: 7.23 us -> 45.7 us  [the longest x31 34.4 us: swapped(): lax.ppermute(value, 'front', [(place, place ^ mask) for place in range(co...]
    dot_general x16 -> x18, matrix products: 43.2 us -> 22.9 us  [the longest x15 12.5 us: product(): jnp.dot(matrix, operand, precision=lax.Precision.HIGH, preferred_element_...]
    all_gather x3 -> x0, local copies, waits for them, and re-layouts: 10.7 us -> none  [local(): all_parents = lax.all_gather(solved, 'front', axis=0, tiled=True)]
    gather x3 -> x0, local copies, waits for them, and re-layouts: 10.6 us -> none  [local(): jnp.take(all_parents, take_index, axis=0)]
    pallas_call x0 -> x6, Pallas kernels: none -> 10.6 us  [the longest x3 5.38 us: parent_solve(): pl.pallas_call(functools.partial(solve_kernel, list(blocks)), out_shape=j...]
  transfers between devices with their start and end apart: 8 -> 39, of which waited for: 8 -> 19; matrix products, arithmetic and copies ran while one was open for 3% -> 13% of each run, Pallas kernels for 0% -> 4%
where the time goes in v1:
time: 153 us; the launch traced here: 156 us
  waiting for transfers between devices  69.6 us (45%)
  starting transfers between devices  45.7 us (30%)
  matrix products  22.9 us (15%)
  Pallas kernels  10.6 us (7%)
  other arithmetic  3.34 us (2%)
  local copies, waits for them, and re-layouts  2.63 us (2%)
    ppermute x31, waiting for transfers between devices, swapped(): lax.ppermute(value, 'front', [(place, place ^ mask) for place in range(co...  48.1 us
    ppermute x31, starting transfers between devices, swapped(): lax.ppermute(value, 'front', [(place, place ^ mask) for place in range(co...  34.4 us
    ppermute x6, waiting for transfers between devices, onward(): return lax.ppermute(value, ('panel', 'front'), pairs)  18.8 us
    dot_general x15, matrix products, product(): jnp.dot(matrix, operand, precision=lax.Precision.HIGH, preferred_element_...  12.5 us
    dot_general x3, matrix products, prepared(): jnp.dot(matrix, operand, precision=lax.Precision.HIGHEST, preferred_eleme...  10.4 us
    ppermute x6, starting transfers between devices, onward(): return lax.ppermute(value, ('panel', 'front'), pairs)  8.69 us
    pallas_call x3, Pallas kernels, parent_solve(): pl.pallas_call(functools.partial(solve_kernel, list(blocks)), out_shape=j...  5.38 us
    pallas_call x3, Pallas kernels, parent_rows(): pl.pallas_call(functools.partial(rows_kernel, wanted), out_shape=[jax.Sha...  5.21 us
  transfers between devices with their start and end apart: 39, of which 19 were waited for; matrix products, arithmetic and copies ran while one was open for 13% of the time, Pallas kernels for 4%

profile of v1, /device:TPU:0, one launch (start us, length us, event | category | flops | bytes accessed | tf_op | source)
XLA Modules:
  0.0 155.8 jit_solution(12865722736550960578)
XLA Ops:
  2.7 2.2 %fusion.9 = f32[768,128]{1,0:T(8,128)S(1)} fusion(f32[1,1,768,768]{3,2,1,0:T(8,128)S(1)} %copy-done, f32[1,1,3,768,128]{4,3,2,1,0:T(8,128)} %param.15), kind=kOutput, calls=%fused_computation.11 | convolution fusion | flops 452984832 | bytes 3145728 | tf_op jit(solution)/shard_map/dot_general | solution.py:67
  6.1 2.7 %collective-permute-start.1 = (f32[384,128]{1,0:T(8,128)S(1)}, f32[384,128]{1,0:T(8,128)S(1)}, u32[]{:S(2)}, u32[]{:S(2)}) collective-permute-start(f32[384,128]{1,0:T(8,128)S(1)} %fusion.51.refs_0_), channel_id=1, source_target_pairs={{0,2},{1,3},{2,0},{3,1},{4,6},{5,7},{6,4},{7,5},{8,10},{9,11},{10,... | collective-permute-start | bytes 589832 | tf_op jit(solution)/shard_map/ppermute | solution.py:16
  8.7 2.5 %collective-permute-start = (f32[384,128]{1,0:T(8,128)S(1)}, f32[384,128]{1,0:T(8,128)S(1)}, u32[]{:S(2)}, u32[]{:S(2)}) collective-permute-start(f32[384,128]{1,0:T(8,128)S(1)} %fusion.51.refs_0_), channel_id=1, source_target_pairs={{0,6},{1,7},{2,4},{3,5},{4,2},{5,3},{6,0},{7,1},{8,14},{9,15},{10,... | collective-permute-start | bytes 589832 | tf_op jit(solution)/shard_map/ppermute | solution.py:16
  11.2 4.1 %fusion.17 = f32[384,768]{1,0:T(8,128)} fusion(f32[1,1,768,768]{3,2,1,0:T(8,128)S(1)} %copy-done, f32[1,1,384,768]{3,2,1,0:T(8,128)S(1)} %copy-done.7, pred[384]{0:T(512)(128)(4,1)S(1)} %iota_compare_fusion), kind=kOutput, calls=%fused_computation.19 | convolution fusion | flops 2718203904 | bytes 4718976 | tf_op jit(solution)/shard_map/dot_general | solution.py:71
  15.3 4.9 %fusion.23 = f32[384,512]{1,0:T(8,128)} fusion(f32[384,768]{1,0:T(8,128)} %fusion.17, f32[1,1,768,512]{3,2,1,0:T(8,128)} %param.14, pred[]{:T(512)S(6)} %gt.3), kind=kOutput, calls=%fused_computation.21 | convolution fusion | flops 1812135936 | bytes 3538945 | tf_op jit(solution)/shard_map/dot_general | solution.py:71
  20.2 2.4 %collective-permute-start.12 = (f32[384,512]{1,0:T(8,128)}, f32[384,512]{1,0:T(8,128)S(1)}, u32[]{:S(2)}, u32[]{:S(2)}) collective-permute-start(f32[384,512]{1,0:T(8,128)} %fusion.23), channel_id=1, source_target_pairs={{0,24},{1,25},{2,26},{3,27},{4,28},{5,29},{6,30},{7,31},{8,0},{9,1... | collective-permute-start | bytes 2359304 | tf_op jit(solution)/shard_map/ppermute | solution.py:27
  24.3 4.8 %collective-permute-done.2.refs_3_ = f32[384,128]{1,0:T(8,128)S(1)} collective-permute-done((f32[384,128]{1,0:T(8,128)S(1)}, f32[384,128]{1,0:T(8,128)S(1)}, u32[]{:S(2)}, u32[]{:S(2)}) %collective-permute-start.2) | collective-permute-done | bytes 196640 | tf_op jit(solution)/shard_map/ppermute | solution.py:16
  36.7 4.2 %collective-permute-done.12 = f32[384,512]{1,0:T(8,128)S(1)} collective-permute-done((f32[384,512]{1,0:T(8,128)}, f32[384,512]{1,0:T(8,128)S(1)}, u32[]{:S(2)}, u32[]{:S(2)}) %collective-permute-start.12) | collective-permute-done | bytes 786464 | tf_op jit(solution)/shard_map/ppermute | solution.py:27
  43.1 3.0 %collective-permute-start.10 = (f32[384,128]{1,0:T(8,128)S(1)}, f32[384,128]{1,0:T(8,128)S(1)}, u32[]{:S(2)}, u32[]{:S(2)}) collective-permute-start(f32[384,128]{1,0:T(8,128)S(1)} %add.45), channel_id=1, source_target_pairs={{0,6},{1,7},{2,4},{3,5},{4,2},{5,3},{6,0},{7,1},{8,14},{9,15},{10,... | collective-permute-start | bytes 589832 | tf_op jit(solution)/shard_map/ppermute | solution.py:16
  48.2 4.9 %collective-permute-done.10 = f32[384,128]{1,0:T(8,128)S(1)} collective-permute-done((f32[384,128]{1,0:T(8,128)S(1)}, f32[384,128]{1,0:T(8,128)S(1)}, u32[]{:S(2)}, u32[]{:S(2)}) %collective-permute-start.10) | collective-permute-done | bytes 196640 | tf_op jit(solution)/shard_map/ppermute | solution.py:16
  53.6 2.8 %collective-permute-start.15 = (f32[384,128]{1,0:T(8,128)S(1)}, f32[384,128]{1,0:T(8,128)S(1)}, u32[]{:S(2)}, u32[]{:S(2)}) collective-permute-start(f32[384,128]{1,0:T(8,128)S(1)} %fusion.65), channel_id=1, source_target_pairs={{0,14},{1,15},{2,12},{3,13},{4,10},{5,11},{6,8},{7,9},{8,22},{9,23... | collective-permute-start | bytes 589832 | tf_op jit(solution)/shard_map/ppermute | solution.py:27
  56.8 6.5 %collective-permute-done.15.refs_1_ = f32[384,128]{1,0:T(8,128)S(1)} collective-permute-done((f32[384,128]{1,0:T(8,128)S(1)}, f32[384,128]{1,0:T(8,128)S(1)}, u32[]{:S(2)}, u32[]{:S(2)}) %collective-permute-start.15) | collective-permute-done | bytes 196640 | tf_op jit(solution)/shard_map/ppermute | solution.py:27
  63.3 4.4 %collective-permute-start.17 = (f32[384,128]{1,0:T(8,128)S(1)}, f32[384,128]{1,0:T(8,128)S(1)}, u32[]{:S(2)}, u32[]{:S(2)}) collective-permute-start(f32[384,128]{1,0:T(8,128)S(1)} %collective-permute-done.15.refs_1_), channel_id=1, source_target_pairs={{0,2},{1,3},{2,0},{3,1},{4,6},{5,7},{6,4},{7,5},{8,10},{9,11},{10,... | collective-permute-start | bytes 589832 | tf_op jit(solution)/shard_map/ppermute | solution.py:16
  67.7 3.5 %collective-permute-start.16 = (f32[384,128]{1,0:T(8,128)S(1)}, f32[384,128]{1,0:T(8,128)S(1)}, u32[]{:S(2)}, u32[]{:S(2)}) collective-permute-start(f32[384,128]{1,0:T(8,128)S(1)} %collective-permute-done.13.refs_0_), channel_id=1, source_target_pairs={{0,2},{1,3},{2,0},{3,1},{4,6},{5,7},{6,4},{7,5},{8,10},{9,11},{10,... | collective-permute-start | bytes 589832 | tf_op jit(solution)/shard_map/ppermute | solution.py:16
  73.1 3.4 %collective-permute-done.16.refs_2_ = f32[384,128]{1,0:T(8,128)S(1)} collective-permute-done((f32[384,128]{1,0:T(8,128)S(1)}, f32[384,128]{1,0:T(8,128)S(1)}, u32[]{:S(2)}, u32[]{:S(2)}) %collective-permute-start.16) | collective-permute-done | bytes 196640 | tf_op jit(solution)/shard_map/ppermute | solution.py:16
  88.2 3.3 %collective-permute-done.23 = f32[384,128]{1,0:T(8,128)S(1)} collective-permute-done((f32[384,128]{1,0:T(8,128)S(1)}, f32[384,128]{1,0:T(8,128)S(1)}, u32[]{:S(2)}, u32[]{:S(2)}) %collective-permute-start.23) | collective-permute-done | bytes 196640 | tf_op jit(solution)/shard_map/ppermute | solution.py:16
  92.6 3.1 %collective-permute-start.25 = (f32[384,128]{1,0:T(8,128)S(1)}, f32[384,128]{1,0:T(8,128)S(1)}, u32[]{:S(2)}, u32[]{:S(2)}) collective-permute-start(f32[384,128]{1,0:T(8,128)S(1)} %add.50), channel_id=1, source_target_pairs={{0,6},{1,7},{2,4},{3,5},{4,2},{5,3},{6,0},{7,1},{8,14},{9,15},{10,... | collective-permute-start | bytes 589832 | tf_op jit(solution)/shard_map/ppermute | solution.py:16
  97.3 5.9 %collective-permute-done.25 = f32[384,128]{1,0:T(8,128)S(1)} collective-permute-done((f32[384,128]{1,0:T(8,128)S(1)}, f32[384,128]{1,0:T(8,128)S(1)}, u32[]{:S(2)}, u32[]{:S(2)}) %collective-permute-start.25) | collective-permute-done | bytes 196640 | tf_op jit(solution)/shard_map/ppermute | solution.py:16
  106.1 8.1 %collective-permute-done.28.refs_1_ = f32[384,128]{1,0:T(8,128)S(1)} collective-permute-done((f32[384,128]{1,0:T(8,128)S(1)}, f32[384,128]{1,0:T(8,128)S(1)}, u32[]{:S(2)}, u32[]{:S(2)}) %collective-permute-start.28) | collective-permute-done | bytes 196640 | tf_op jit(solution)/shard_map/ppermute | solution.py:27
  114.2 4.8 %collective-permute-start.30 = (f32[384,128]{1,0:T(8,128)S(1)}, f32[384,128]{1,0:T(8,128)S(1)}, u32[]{:S(2)}, u32[]{:S(2)}) collective-permute-start(f32[384,128]{1,0:T(8,128)S(1)} %collective-permute-done.28.refs_1_), channel_id=1, source_target_pairs={{0,2},{1,3},{2,0},{3,1},{4,6},{5,7},{6,4},{7,5},{8,10},{9,11},{10,... | collective-permute-start | bytes 589832 | tf_op jit(solution)/shard_map/ppermute | solution.py:16
  119.7 5.0 %collective-permute-done.30.refs_3_ = f32[384,128]{1,0:T(8,128)S(1)} collective-permute-done((f32[384,128]{1,0:T(8,128)S(1)}, f32[384,128]{1,0:T(8,128)S(1)}, u32[]{:S(2)}, u32[]{:S(2)}) %collective-permute-start.30) | collective-permute-done | bytes 196640 | tf_op jit(solution)/shard_map/ppermute | solution.py:16
  124.7 3.5 %collective-permute-done.29.refs_2_ = f32[384,128]{1,0:T(8,128)S(1)} collective-permute-done((f32[384,128]{1,0:T(8,128)S(1)}, f32[384,128]{1,0:T(8,128)S(1)}, u32[]{:S(2)}, u32[]{:S(2)}) %collective-permute-start.29) | collective-permute-done | bytes 196640 | tf_op jit(solution)/shard_map/ppermute | solution.py:16
  140.1 3.3 %collective-permute-done.36 = f32[384,128]{1,0:T(8,128)S(1)} collective-permute-done((f32[384,128]{1,0:T(8,128)S(1)}, f32[384,128]{1,0:T(8,128)S(1)}, u32[]{:S(2)}, u32[]{:S(2)}) %collective-permute-start.36) | collective-permute-done | bytes 196640 | tf_op jit(solution)/shard_map/ppermute | solution.py:16
  147.3 6.7 %collective-permute-done.38 = f32[384,128]{1,0:T(8,128)S(1)} collective-permute-done((f32[384,128]{1,0:T(8,128)S(1)}, f32[384,128]{1,0:T(8,128)S(1)}, u32[]{:S(2)}, u32[]{:S(2)}) %collective-permute-start.38) | collective-permute-done | bytes 196640 | tf_op jit(solution)/shard_map/ppermute | solution.py:16
  (118 shorter events, 54.7 us)
Async XLA Ops:
  5.6 23.6 %collective-permute-start.3 = (f32[384,128]{1,0:T(8,128)S(1)}, f32[384,128]{1,0:T(8,128)S(1)}, u32[]{:S(2)}, u32[]{:S(2)}) collective-permute-start(f32[384,128]{1,0:T(8,128)S(1)} %fusion.51.refs_0_), channel_id=1, source_target_pairs={{0,1},{1,0},{2,3},{3,2},{4,5},{5,4},{6,7},{7,6},{8,9},{9,8},{10,11... | collective-permute-start | bytes 589832 | tf_op jit(solution)/shard_map/ppermute | solution.py:16
  6.1 17.7 %collective-permute-start.1 = (f32[384,128]{1,0:T(8,128)S(1)}, f32[384,128]{1,0:T(8,128)S(1)}, u32[]{:S(2)}, u32[]{:S(2)}) collective-permute-start(f32[384,128]{1,0:T(8,128)S(1)} %fusion.51.refs_0_), channel_id=1, source_target_pairs={{0,2},{1,3},{2,0},{3,1},{4,6},{5,7},{6,4},{7,5},{8,10},{9,11},{10,... | collective-permute-start | bytes 589832 | tf_op jit(solution)/shard_map/ppermute | solution.py:16
  8.7 13.9 %collective-permute-start = (f32[384,128]{1,0:T(8,128)S(1)}, f32[384,128]{1,0:T(8,128)S(1)}, u32[]{:S(2)}, u32[]{:S(2)}) collective-permute-start(f32[384,128]{1,0:T(8,128)S(1)} %fusion.51.refs_0_), channel_id=1, source_target_pairs={{0,6},{1,7},{2,4},{3,5},{4,2},{5,3},{6,0},{7,1},{8,14},{9,15},{10,... | collective-permute-start | bytes 589832 | tf_op jit(solution)/shard_map/ppermute | solution.py:16
  20.2 20.7 %collective-permute-start.12 = (f32[384,512]{1,0:T(8,128)}, f32[384,512]{1,0:T(8,128)S(1)}, u32[]{:S(2)}, u32[]{:S(2)}) collective-permute-start(f32[384,512]{1,0:T(8,128)} %fusion.23), channel_id=1, source_target_pairs={{0,24},{1,25},{2,26},{3,27},{4,28},{5,29},{6,30},{7,31},{8,0},{9,1... | collective-permute-start | bytes 2359304 | tf_op jit(solution)/shard_map/ppermute | solution.py:27
  34.3 18.9 %collective-permute-start.11 = (f32[384,256]{1,0:T(8,128)S(1)}, f32[384,256]{1,0:T(8,128)S(1)}, u32[]{:S(2)}, u32[]{:S(2)}) collective-permute-start(f32[384,256]{1,0:T(8,128)S(1)} %fusion.57), channel_id=1, source_target_pairs={{0,24},{1,25},{2,26},{3,27},{4,28},{5,29},{6,30},{7,31},{8,0},{9,1... | collective-permute-start | bytes 1179656 | tf_op jit(solution)/shard_map/ppermute | solution.py:27
  43.1 10.0 %collective-permute-start.10 = (f32[384,128]{1,0:T(8,128)S(1)}, f32[384,128]{1,0:T(8,128)S(1)}, u32[]{:S(2)}, u32[]{:S(2)}) collective-permute-start(f32[384,128]{1,0:T(8,128)S(1)} %add.45), channel_id=1, source_target_pairs={{0,6},{1,7},{2,4},{3,5},{4,2},{5,3},{6,0},{7,1},{8,14},{9,15},{10,... | collective-permute-start | bytes 589832 | tf_op jit(solution)/shard_map/ppermute | solution.py:16
  53.6 9.7 %collective-permute-start.15 = (f32[384,128]{1,0:T(8,128)S(1)}, f32[384,128]{1,0:T(8,128)S(1)}, u32[]{:S(2)}, u32[]{:S(2)}) collective-permute-start(f32[384,128]{1,0:T(8,128)S(1)} %fusion.65), channel_id=1, source_target_pairs={{0,14},{1,15},{2,12},{3,13},{4,10},{5,11},{6,8},{7,9},{8,22},{9,23... | collective-permute-start | bytes 589832 | tf_op jit(solution)/shard_map/ppermute | solution.py:27
  56.4 11.3 %collective-permute-start.13 = (f32[384,128]{1,0:T(8,128)S(1)}, f32[384,128]{1,0:T(8,128)S(1)}, u32[]{:S(2)}, u32[]{:S(2)}) collective-permute-start(f32[384,128]{1,0:T(8,128)S(1)} %fusion.65), channel_id=1, source_target_pairs={{0,8},{1,9},{2,10},{3,11},{4,12},{5,13},{6,14},{7,15},{8,16},{9,17... | collective-permute-start | bytes 589832 | tf_op jit(solution)/shard_map/ppermute | solution.py:27
  63.3 9.8 %collective-permute-start.17 = (f32[384,128]{1,0:T(8,128)S(1)}, f32[384,128]{1,0:T(8,128)S(1)}, u32[]{:S(2)}, u32[]{:S(2)}) collective-permute-start(f32[384,128]{1,0:T(8,128)S(1)} %collective-permute-done.15.refs_1_), channel_id=1, source_target_pairs={{0,2},{1,3},{2,0},{3,1},{4,6},{5,7},{6,4},{7,5},{8,10},{9,11},{10,... | collective-permute-start | bytes 589832 | tf_op jit(solution)/shard_map/ppermute | solution.py:16
  67.7 8.8 %collective-permute-start.16 = (f32[384,128]{1,0:T(8,128)S(1)}, f32[384,128]{1,0:T(8,128)S(1)}, u32[]{:S(2)}, u32[]{:S(2)}) collective-permute-start(f32[384,128]{1,0:T(8,128)S(1)} %collective-permute-done.13.refs_0_), channel_id=1, source_target_pairs={{0,2},{1,3},{2,0},{3,1},{4,6},{5,7},{6,4},{7,5},{8,10},{9,11},{10,... | collective-permute-start | bytes 589832 | tf_op jit(solution)/shard_map/ppermute | solution.py:16
  80.6 7.7 %collective-permute-start.14 = (f32[512,128]{1,0:T(8,128)S(1)}, f32[512,128]{1,0:T(8,128)S(1)}, u32[]{:S(2)}, u32[]{:S(2)}) collective-permute-start(f32[512,128]{1,0:T(8,128)S(1)} %slice.70), channel_id=1, source_target_pairs={{0,8},{8,16},{16,24},{1,9},{9,17},{17,25},{2,10},{10,18},{18,26},{... | collective-permute-start | bytes 786440 | tf_op jit(solution)/shard_map/ppermute | solution.py:260
  83.6 7.9 %collective-permute-start.23 = (f32[384,128]{1,0:T(8,128)S(1)}, f32[384,128]{1,0:T(8,128)S(1)}, u32[]{:S(2)}, u32[]{:S(2)}) collective-permute-start(f32[384,128]{1,0:T(8,128)S(1)} %get-tuple-element.23), channel_id=1, source_target_pairs={{0,2},{1,3},{2,0},{3,1},{4,6},{5,7},{6,4},{7,5},{8,10},{9,11},{10,... | collective-permute-start | bytes 589832 | tf_op jit(solution)/shard_map/ppermute | solution.py:16
  85.7 11.6 %collective-permute-start.24 = (f32[384,128]{1,0:T(8,128)S(1)}, f32[384,128]{1,0:T(8,128)S(1)}, u32[]{:S(2)}, u32[]{:S(2)}) collective-permute-start(f32[384,128]{1,0:T(8,128)S(1)} %get-tuple-element.26), channel_id=1, source_target_pairs={{0,2},{1,3},{2,0},{3,1},{4,6},{5,7},{6,4},{7,5},{8,10},{9,11},{10,... | collective-permute-start | bytes 589832 | tf_op jit(solution)/shard_map/ppermute | solution.py:16
  92.6 10.7 %collective-permute-start.25 = (f32[384,128]{1,0:T(8,128)S(1)}, f32[384,128]{1,0:T(8,128)S(1)}, u32[]{:S(2)}, u32[]{:S(2)}) collective-permute-start(f32[384,128]{1,0:T(8,128)S(1)} %add.50), channel_id=1, source_target_pairs={{0,6},{1,7},{2,4},{3,5},{4,2},{5,3},{6,0},{7,1},{8,14},{9,15},{10,... | collective-permute-start | bytes 589832 | tf_op jit(solution)/shard_map/ppermute | solution.py:16
  103.7 10.5 %collective-permute-start.28 = (f32[384,128]{1,0:T(8,128)S(1)}, f32[384,128]{1,0:T(8,128)S(1)}, u32[]{:S(2)}, u32[]{:S(2)}) collective-permute-start(f32[384,128]{1,0:T(8,128)S(1)} %fusion.64), channel_id=1, source_target_pairs={{0,14},{1,15},{2,12},{3,13},{4,10},{5,11},{6,8},{7,9},{8,22},{9,23... | collective-permute-start | bytes 589832 | tf_op jit(solution)/shard_map/ppermute | solution.py:27
  105.0 14.0 %collective-permute-start.26 = (f32[384,128]{1,0:T(8,128)S(1)}, f32[384,128]{1,0:T(8,128)S(1)}, u32[]{:S(2)}, u32[]{:S(2)}) collective-permute-start(f32[384,128]{1,0:T(8,128)S(1)} %fusion.64), channel_id=1, source_target_pairs={{0,8},{1,9},{2,10},{3,11},{4,12},{5,13},{6,14},{7,15},{8,16},{9,17... | collective-permute-start | bytes 589832 | tf_op jit(solution)/shard_map/ppermute | solution.py:27
  114.2 10.5 %collective-permute-start.30 = (f32[384,128]{1,0:T(8,128)S(1)}, f32[384,128]{1,0:T(8,128)S(1)}, u32[]{:S(2)}, u32[]{:S(2)}) collective-permute-start(f32[384,128]{1,0:T(8,128)S(1)} %collective-permute-done.28.refs_1_), channel_id=1, source_target_pairs={{0,2},{1,3},{2,0},{3,1},{4,6},{5,7},{6,4},{7,5},{8,10},{9,11},{10,... | collective-permute-start | bytes 589832 | tf_op jit(solution)/shard_map/ppermute | solution.py:16
  119.0 9.2 %collective-permute-start.29 = (f32[384,128]{1,0:T(8,128)S(1)}, f32[384,128]{1,0:T(8,128)S(1)}, u32[]{:S(2)}, u32[]{:S(2)}) collective-permute-start(f32[384,128]{1,0:T(8,128)S(1)} %collective-permute-done.26.refs_0_), channel_id=1, source_target_pairs={{0,2},{1,3},{2,0},{3,1},{4,6},{5,7},{6,4},{7,5},{8,10},{9,11},{10,... | collective-permute-start | bytes 589832 | tf_op jit(solution)/shard_map/ppermute | solution.py:16
  119.2 9.1 %collective-permute-start.32 = (f32[384,128]{1,0:T(8,128)S(1)}, f32[384,128]{1,0:T(8,128)S(1)}, u32[]{:S(2)}, u32[]{:S(2)}) collective-permute-start(f32[384,128]{1,0:T(8,128)S(1)} %collective-permute-done.28.refs_1_), channel_id=1, source_target_pairs={{0,1},{1,0},{2,3},{3,2},{4,5},{5,4},{6,7},{7,6},{8,9},{9,8},{10,11... | collective-permute-start | bytes 589832 | tf_op jit(solution)/shard_map/ppermute | solution.py:16
  119.2 9.1 %collective-permute-start.31 = (f32[384,128]{1,0:T(8,128)S(1)}, f32[384,128]{1,0:T(8,128)S(1)}, u32[]{:S(2)}, u32[]{:S(2)}) collective-permute-start(f32[384,128]{1,0:T(8,128)S(1)} %collective-permute-done.26.refs_0_), channel_id=1, source_target_pairs={{0,1},{1,0},{2,3},{3,2},{4,5},{5,4},{6,7},{7,6},{8,9},{9,8},{10,11... | collective-permute-start | bytes 589832 | tf_op jit(solution)/shard_map/ppermute | solution.py:16
  132.4 7.7 %collective-permute-start.27 = (f32[512,128]{1,0:T(8,128)S(1)}, f32[512,128]{1,0:T(8,128)S(1)}, u32[]{:S(2)}, u32[]{:S(2)}) collective-permute-start(f32[512,128]{1,0:T(8,128)S(1)} %slice.74), channel_id=1, source_target_pairs={{0,8},{8,16},{16,24},{1,9},{9,17},{17,25},{2,10},{10,18},{18,26},{... | collective-permute-start | bytes 786440 | tf_op jit(solution)/shard_map/ppermute | solution.py:260
  135.5 7.9 %collective-permute-start.36 = (f32[384,128]{1,0:T(8,128)S(1)}, f32[384,128]{1,0:T(8,128)S(1)}, u32[]{:S(2)}, u32[]{:S(2)}) collective-permute-start(f32[384,128]{1,0:T(8,128)S(1)} %get-tuple-element.29), channel_id=1, source_target_pairs={{0,2},{1,3},{2,0},{3,1},{4,6},{5,7},{6,4},{7,5},{8,10},{9,11},{10,... | collective-permute-start | bytes 589832 | tf_op jit(solution)/shard_map/ppermute | solution.py:16
  137.3 10.0 %collective-permute-start.37 = (f32[384,128]{1,0:T(8,128)S(1)}, f32[384,128]{1,0:T(8,128)S(1)}, u32[]{:S(2)}, u32[]{:S(2)}) collective-permute-start(f32[384,128]{1,0:T(8,128)S(1)} %get-tuple-element.32), channel_id=1, source_target_pairs={{0,2},{1,3},{2,0},{3,1},{4,6},{5,7},{6,4},{7,5},{8,10},{9,11},{10,... | collective-permute-start | bytes 589832 | tf_op jit(solution)/shard_map/ppermute | solution.py:16
  144.4 9.6 %collective-permute-start.38 = (f32[384,128]{1,0:T(8,128)S(1)}, f32[384,128]{1,0:T(8,128)S(1)}, u32[]{:S(2)}, u32[]{:S(2)}) collective-permute-start(f32[384,128]{1,0:T(8,128)S(1)} %add.55), channel_id=1, source_target_pairs={{0,6},{1,7},{2,4},{3,5},{4,2},{5,3},{6,0},{7,1},{8,14},{9,15},{10,... | collective-permute-start | bytes 589832 | tf_op jit(solution)/shard_map/ppermute | solution.py:16
  (28 other events, 145.3 us)

commit v2 on v1

--- a/solution.py
+++ b/solution.py
@@ -53,22 +53,15 @@
 def delivered(parts, masks):
     parts = dict(parts)
     span = offsets(masks)
-    first = None
     for step in range(len(masks) - 1, -1, -1):
         mask = masks[step]
         for offset in span[2 ** step - 1 :: -1]:
-            received = swapped(parts.pop(offset ^ mask), mask)
-            first = received if first is None else first
-            parts[offset] = parts[offset] + received
-    return parts[0], first
+            parts[offset] = parts[offset] + swapped(parts.pop(offset ^ mask), mask)
+    return parts[0]
 
 
 def product(matrix, operand):
     return jnp.dot(matrix, operand, precision=lax.Precision.HIGH, preferred_element_type=jnp.float32)
-
-
-def prepared(matrix, operand):
-    return jnp.dot(matrix, operand, precision=lax.Precision.HIGHEST, preferred_element_type=jnp.float32)
 
 
 def halves(value):
@@ -91,16 +84,17 @@
     return lax.optimization_barrier((value, event))[0]
 
 
-def solve_kernel(offsets_in, place, parents, rows, high, low, sources, *refs):
-    blocks, out, rhs = refs[:-2], refs[-2], refs[-1]
-    rhs[...] = sources[...]
-    extent = (rhs.shape[0], rows.shape[1])
+def subtract_rows(rhs, offsets_in, blocks, place, parents, counts, rows):
+    cap = rows.shape[1]
+    extent = (rhs.shape[0], cap)
     for offset, block in zip(offsets_in, blocks):
         leaf = place[0] ^ offset
 
         @pl.when(parents[0, leaf] == place[0])
         def _():
-            choice = lax.broadcasted_iota(jnp.int32, extent, 0) == rows[pl.ds(leaf, 1), :]
+            slot = lax.broadcasted_iota(jnp.int32, (1, cap), 1)
+            targets = jnp.where(slot < counts[0, leaf], rows[pl.ds(leaf, 1), :], -1)
+            choice = lax.broadcasted_iota(jnp.int32, extent, 0) == targets
             pair = jnp.dot(
                 jnp.where(choice, 1.0, 0.0).astype(jnp.bfloat16),
                 side_by_side(block[...]),
@@ -108,6 +102,17 @@
             )
             rhs[...] -= summed(pair)
 
+
+def early_kernel(offsets_in, tick, place, parents, counts, rows, sources, *refs):
+    blocks, rhs = refs[:-1], refs[-1]
+    rhs[...] = sources[tick]
+    subtract_rows(rhs, offsets_in, blocks, place, parents, counts, rows)
+
+
+def solve_kernel(offsets_in, place, parents, counts, rows, high, low, partial_rhs, *refs):
+    blocks, out, rhs = refs[:-2], refs[-2], refs[-1]
+    rhs[...] = partial_rhs[...]
+    subtract_rows(rhs, offsets_in, blocks, place, parents, counts, rows)
     both = side_by_side(rhs[...])
     columns = out.shape[1]
     out[...] = summed(jnp.dot(high[...], both, preferred_element_type=jnp.float32)) + jnp.dot(
@@ -115,25 +120,41 @@
     )
 
 
-def parent_solve(place, parents, rows, high, low, sources, blocks):
-    order = sources.shape[0]
-    depth = sum(block.shape[0] for block in blocks.values())
+def rows_subtracted(place, parents, counts, rows, sources, tick, blocks):
+    smem = pl.BlockSpec(memory_space=pltpu.SMEM)
+    vmem = pl.BlockSpec(memory_space=pltpu.VMEM)
+    order, columns = sources.shape[1:]
+    return pl.pallas_call(
+        functools.partial(early_kernel, list(blocks), tick),
+        out_shape=jax.ShapeDtypeStruct((order, columns), jnp.float32),
+        in_specs=[smem] * 3 + [vmem] * (2 + len(blocks)),
+        out_specs=vmem,
+        compiler_params=pltpu.CompilerParams(vmem_limit_bytes=VMEM_BYTES),
+        cost_estimate=pl.CostEstimate(
+            flops=4 * order * rows.shape[1] * columns * len(blocks),
+            bytes_accessed=8 * order * columns,
+            transcendentals=0,
+        ),
+        name="rows_subtracted",
+    )(place, parents, counts, rows, sources, *blocks.values())
+
+
+def parent_solve(place, parents, counts, rows, high, low, partial_rhs, blocks):
+    order, columns = partial_rhs.shape
     smem = pl.BlockSpec(memory_space=pltpu.SMEM)
     vmem = pl.BlockSpec(memory_space=pltpu.VMEM)
     return pl.pallas_call(
         functools.partial(solve_kernel, list(blocks)),
-        out_shape=jax.ShapeDtypeStruct(sources.shape, jnp.float32),
-        in_specs=[smem] * 2 + [vmem] * (4 + len(blocks)),
+        out_shape=jax.ShapeDtypeStruct(partial_rhs.shape, jnp.float32),
+        in_specs=[smem] * 3 + [vmem] * (4 + len(blocks)),
         out_specs=vmem,
-        scratch_shapes=[pltpu.VMEM(sources.shape, jnp.float32)],
+        scratch_shapes=[pltpu.VMEM(partial_rhs.shape, jnp.float32)],
         compiler_params=pltpu.CompilerParams(vmem_limit_bytes=VMEM_BYTES),
         cost_estimate=pl.CostEstimate(
-            flops=8 * order * order * sources.shape[1],
-            bytes_accessed=4 * order * (order + 256) + 512 * depth,
-            transcendentals=0,
+            flops=8 * order * order * columns, bytes_accessed=4 * order * (order + 256), transcendentals=0
         ),
         name="parent_solve",
-    )(place, parents, rows, high, low, sources, *blocks.values())
+    )(place, parents, counts, rows, high, low, partial_rhs, *blocks.values())
 
 
 def rows_kernel(offsets_out, place, parents, counts, rows, own, other, *refs):
@@ -214,56 +235,61 @@
     place = myself.astype(jnp.int32).reshape(1)
     masks = cube_masks(fronts)
     span = offsets(masks)
-    own_count = lax.dynamic_index_in_dim(update_count[0], myself, 0, keepdims=False)
-    own_live = (jnp.arange(row_ids.shape[1], dtype=jnp.int32) < own_count)[:, None]
-
     def edge(value):
         return value[leaf_order - iface_rows :]
 
     sources = leaf_sources[0, 0]
     partial_solution = product(inverse, sources[0])
-    update = jnp.where(own_live, product(upward, partial_solution), 0.0)
+    update = product(upward, partial_solution)
     held = spread({0: update}, masks)
     parent_high, parent_low = halves(parent_inv[0, 0])
 
     later = jnp.concatenate([sources[tick] for tick in range(1, ticks)], axis=1)
-    along = jnp.where(own_live, prepared(upward, inverse), 0.0)
-    through = jnp.where(lax.axis_index("panel") > 0, prepared(along, coupling), 0.0)
+    along = product(upward, inverse)
+    through = jnp.where(lax.axis_index("panel") > 0, product(along, coupling), 0.0)
     next_through = onward(through, -1, 0)
     next_sources = onward(product(along, later), -1, 0)
-    next_descended = prepared(next_through, edge(downward))
+    next_descended = product(next_through, edge(downward))
     own_later = product(inverse, later)
 
-    leaf_list = []
-    parent_list = []
-    interface = None
+    tables = (place, parent_of, update_count, row_ids)
+    leaf_out = jnp.zeros(sources.shape, jnp.float32)
+    parent_out = jnp.zeros(parent_sources.shape[2:], jnp.float32)
+    leaf_now = None
     for tick in range(ticks):
-        blocks = {offset: held[offset] for offset in span}
-        blocks.update({offset ^ TWIN: swapped(held[offset], TWIN) for offset in span})
-        solved = parent_solve(
-            place, parent_of, row_ids, parent_high, parent_low, parent_sources[0, 0, tick], blocks
-        )
-        parent_list.append(solved)
-        parts = parent_rows(place, parent_of, update_count, row_ids, solved, swapped(solved, TWIN), span)
-        descended, first = delivered(parts, masks)
+        early = {}
+        for offset in span[:-1]:
+            early[offset] = held[offset]
+            early[offset ^ TWIN] = swapped(held[offset], TWIN)
+        late = {span[-1]: held[span[-1]], span[-1] ^ TWIN: swapped(held[span[-1]], TWIN)}
+        partial_rhs = rows_subtracted(*tables, parent_sources[0, 0], tick, early)
+        solved = parent_solve(*tables, parent_high, parent_low, partial_rhs, late)
+        other = swapped(solved, TWIN)
+        parts = parent_rows(*tables, solved, other, span[-1:])
+        parts.update(parent_rows(*tables, after(solved, parts[span[-1]]), other, span[:-1]))
+        descended = delivered(parts, masks)
         at = slice((tick - 1) * columns, tick * columns)
         if tick > 0:
-            arrived = after(interface, first)
-            partial_solution = own_later[:, at] + product(inverse, product(coupling, arrived))
+            leaving = after(edge(leaf_now), parts[0])
+            interface = lax.ppermute(leaving, "panel", [(spot, spot + 1) for spot in range(panels - 1)])
+            partial_solution = own_later[:, at] + product(inverse, product(coupling, interface))
         if tick + 1 < ticks:
             at = slice(tick * columns, (tick + 1) * columns)
             base = next_sources[:, at] + product(next_through, edge(partial_solution))
             update = base - product(next_descended, descended)
-            moved = onward(update, 1, 0)
-            held = spread({0: moved, masks[0]: onward(update, 1, masks[0])}, masks[1:])
-            leaf_now = partial_solution - product(downward, after(descended, moved))
-            interface = lax.ppermute(edge(leaf_now), "panel", [(spot, spot + 1) for spot in range(panels - 1)])
+            moved = {offset: onward(update, 1, offset) for offset in masks}
+            moved[0] = onward(update, 1, 0)
+            held = dict(moved)
+            for step, mask in enumerate(masks):
+                for offset in offsets(masks[:step]):
+                    if offset ^ mask not in held:
+                        held[offset ^ mask] = swapped(held[offset], mask)
+            leaf_now = partial_solution - product(downward, after(descended, moved[masks[0]]))
         else:
             leaf_now = partial_solution - product(downward, descended)
-        leaf_list.append(leaf_now)
-    leaf_out = jnp.stack(leaf_list, axis=0)[None, None]
-    parent_out = jnp.stack(parent_list, axis=0)[None, None]
-    return (leaf_out, parent_out)
+        leaf_out = lax.dynamic_update_index_in_dim(leaf_out, leaf_now, tick, 0)
+        parent_out = lax.dynamic_update_index_in_dim(parent_out, solved, tick, 0)
+    return (leaf_out[None, None], parent_out[None, None])
 
 
 def solution(mesh):

time: 153 us -> 149 us (0.974); the launches traced: 156 us -> 146 us
  waiting for transfers between devices: 69.6 us -> 52.5 us
  local copies, waits for them, and re-layouts: 2.63 us -> 6.8 us
  starting transfers between devices: 45.7 us -> 49.2 us
  Pallas kernels: 10.6 us -> 13.9 us
  other arithmetic: 3.34 us -> 1.5 us
  matrix products: 22.9 us -> 21.1 us
    ppermute x31 -> x29, waiting for transfers between devices: 48.1 us -> 29.1 us  [swapped(): lax.ppermute(value, 'front', [(place, place ^ mask) for place in range(co...]
    ppermute x31 -> x29, starting transfers between devices: 34.4 us -> 22.9 us  [swapped(): lax.ppermute(value, 'front', [(place, place ^ mask) for place in range(co...]
    dot_general x3 -> x0, matrix products: 10.4 us -> none  [prepared(): jnp.dot(matrix, operand, precision=lax.Precision.HIGHEST, preferred_eleme...]
    ppermute x6 -> x8, starting transfers between devices: 8.69 us -> 18.3 us  [onward(): return lax.ppermute(value, ('panel', 'front'), pairs)]
    dot_general x15 -> x18, matrix products: 12.5 us -> 21.1 us  [product(): jnp.dot(matrix, operand, precision=lax.Precision.HIGH, preferred_element_...]
    unnamed x26 -> x38, local copies, waits for them, and re-layouts: 1.07 us -> 6.5 us
    ppermute x2, starting transfers between devices: 2.61 us -> 8.02 us  [local(): lax.ppermute(leaving, 'panel', [(spot, spot + 1) for spot in range(panels...]
    pallas_call x0 -> x3, Pallas kernels: none -> 3.85 us  [rows_subtracted(): pl.pallas_call(functools.partial(early_kernel, list(blocks), tick), out_s...]
  transfers between devices with their start and end apart: 39 -> 39, of which waited for: 19 -> 21; matrix products, arithmetic and copies ran while one was open for 13% -> 12% of each run, Pallas kernels for 4% -> 6%
where the time goes in v2:
time: 149 us; the launch traced here: 146 us
  waiting for transfers between devices  52.5 us (35%)
  starting transfers between devices  49.2 us (33%)
  matrix products  21.1 us (14%)
  Pallas kernels  13.9 us (9%)
  local copies, waits for them, and re-layouts  6.8 us (5%)
  other arithmetic  1.5 us (1%)
    ppermute x29, waiting for transfers between devices, swapped(): lax.ppermute(value, 'front', [(place, place ^ mask) for place in range(co...  29.1 us
    ppermute x29, starting transfers between devices, swapped(): lax.ppermute(value, 'front', [(place, place ^ mask) for place in range(co...  22.9 us
    ppermute x8, waiting for transfers between devices, onward(): return lax.ppermute(value, ('panel', 'front'), pairs)  21.1 us
    dot_general x18, matrix products, product(): jnp.dot(matrix, operand, precision=lax.Precision.HIGH, preferred_element_...  21.1 us
    ppermute x8, starting transfers between devices, onward(): return lax.ppermute(value, ('panel', 'front'), pairs)  18.3 us
    ppermute x2, starting transfers between devices, local(): lax.ppermute(leaving, 'panel', [(spot, spot + 1) for spot in range(panels...  8.02 us
    unnamed x38, local copies, waits for them, and re-layouts  6.5 us
    pallas_call x3, Pallas kernels, parent_solve(): pl.pallas_call(functools.partial(solve_kernel, list(blocks)), out_shape=j...  5.8 us
  transfers between devices with their start and end apart: 39, of which 21 were waited for; matrix products, arithmetic and copies ran while one was open for 12% of the time, Pallas kernels for 6%

profile of v2, /device:TPU:0, one launch (start us, length us, event | category | flops | bytes accessed | tf_op | source)
XLA Modules:
  0.0 146.2 jit_solution(14276327112221342249)
XLA Ops:
  2.3 2.1 %fusion.9 = f32[768,128]{1,0:T(8,128)S(1)} fusion(f32[1,1,768,768]{3,2,1,0:T(8,128)S(1)} %copy-done, f32[1,1,3,768,128]{4,3,2,1,0:T(8,128)} %param.15), kind=kOutput, calls=%fused_computation.11 | convolution fusion | flops 452984832 | bytes 3145728 | tf_op jit(solution)/shard_map/dot_general | solution.py:64
  6.4 3.0 %collective-permute-start.3 = (f32[384,128]{1,0:T(8,128)}, f32[384,128]{1,0:T(8,128)}, u32[]{:S(2)}, u32[]{:S(2)}) collective-permute-start(f32[384,128]{1,0:T(8,128)} %fusion.46.refs_0_), channel_id=1, source_target_pairs={{0,2},{1,3},{2,0},{3,1},{4,6},{5,7},{6,4},{7,5},{8,10},{9,11},{10,... | collective-permute-start | bytes 589832 | tf_op jit(solution)/shard_map/ppermute | solution.py:16
  9.5 2.5 %collective-permute-start.1 = (f32[384,128]{1,0:T(8,128)}, f32[384,128]{1,0:T(8,128)}, u32[]{:S(2)}, u32[]{:S(2)}) collective-permute-start(f32[384,128]{1,0:T(8,128)} %fusion.46.refs_0_), channel_id=1, source_target_pairs={{0,6},{1,7},{2,4},{3,5},{4,2},{5,3},{6,0},{7,1},{8,14},{9,15},{10,... | collective-permute-start | bytes 589832 | tf_op jit(solution)/shard_map/ppermute | solution.py:16
  13.7 7.5 %collective-permute-done.1.refs_2_ = f32[384,128]{1,0:T(8,128)} collective-permute-done((f32[384,128]{1,0:T(8,128)}, f32[384,128]{1,0:T(8,128)}, u32[]{:S(2)}, u32[]{:S(2)}) %collective-permute-start.1) | collective-permute-done | bytes 196640 | tf_op jit(solution)/shard_map/ppermute | solution.py:16
  21.8 2.1 %fusion.20 = f32[384,512]{1,0:T(8,128)} fusion(f32[384,768]{1,0:T(8,128)S(1)} %fusion.7, f32[1,1,768,512]{3,2,1,0:T(8,128)S(1)} %copy-done.8, pred[]{:T(512)S(6)} %gt.3), kind=kOutput, calls=%fused_computation.20 | convolution fusion | flops 906166272 | bytes 3538945 | tf_op jit(solution)/shard_map/dot_general | solution.py:64
  23.9 2.5 %collective-permute-start.12 = (f32[384,512]{1,0:T(8,128)}, f32[384,512]{1,0:T(8,128)}, u32[]{:S(2)}, u32[]{:S(2)}) collective-permute-start(f32[384,512]{1,0:T(8,128)} %fusion.20), channel_id=1, source_target_pairs={{0,24},{1,25},{2,26},{3,27},{4,28},{5,29},{6,30},{7,31},{8,0},{9,1... | collective-permute-start | bytes 2359304 | tf_op jit(solution)/shard_map/ppermute | solution.py:27
  32.5 2.3 %parent_solve.3.own = f32[768,128]{1,0:T(8,128)S(1)} custom-call(s32[1]{0:T(128)} %bitcast.2.place, s32[1,8]{1,0:T(1,128)S(1)} %copy-done.3, s32[1,8]{1,0:T(1,128)S(1)} %copy-done.4, s32[8,384]{1,0:T(8,128)S(1)} %bitcast.124, bf16[768,768]{1,0:T(8,128)(2,1)S(1)} %copy-done.1, bf16[768,768]{1,0:T(8,128)(2,1)S(1)} %get-tuple-element.34.low, ...), custom_call_target="tpu_custom_call" | custom-call | flops 603979776 | bytes 3145728 | tf_op jit(solution)/shard_map/parent_solve/pallas_call | solution.py:146
  36.7 3.2 %collective-permute-start.11 = (f32[384,256]{1,0:T(8,128)S(1)}, f32[384,256]{1,0:T(8,128)S(1)}, u32[]{:S(2)}, u32[]{:S(2)}) collective-permute-start(f32[384,256]{1,0:T(8,128)S(1)} %fusion.52), channel_id=1, source_target_pairs={{0,24},{1,25},{2,26},{3,27},{4,28},{5,29},{6,30},{7,31},{8,0},{9,1... | collective-permute-start | bytes 1179656 | tf_op jit(solution)/shard_map/ppermute | solution.py:27
  40.7 3.7 %collective-permute-done.12 = f32[384,512]{1,0:T(8,128)} collective-permute-done((f32[384,512]{1,0:T(8,128)}, f32[384,512]{1,0:T(8,128)}, u32[]{:S(2)}, u32[]{:S(2)}) %collective-permute-start.12) | collective-permute-done | bytes 786464 | tf_op jit(solution)/shard_map/ppermute | solution.py:27
  52.5 1.9 %collective-permute-done.8 = f32[384,128]{1,0:T(8,128)S(1)} collective-permute-done((f32[384,128]{1,0:T(8,128)S(1)}, f32[384,128]{1,0:T(8,128)S(1)}, u32[]{:S(2)}, u32[]{:S(2)}) %collective-permute-start.8) | collective-permute-done | bytes 196640 | tf_op jit(solution)/shard_map/ppermute | solution.py:16
  54.4 2.3 %collective-permute-done.10 = f32[384,128]{1,0:T(8,128)S(1)} collective-permute-done((f32[384,128]{1,0:T(8,128)S(1)}, f32[384,128]{1,0:T(8,128)S(1)}, u32[]{:S(2)}, u32[]{:S(2)}) %collective-permute-start.10) | collective-permute-done | bytes 196640 | tf_op jit(solution)/shard_map/ppermute | solution.py:16
  57.2 5.0 %collective-permute-start.13 = (f32[384,128]{1,0:T(8,128)S(1)}, f32[384,128]{1,0:T(8,128)S(1)}, u32[]{:S(2)}, u32[]{:S(2)}) collective-permute-start(f32[384,128]{1,0:T(8,128)S(1)} %fusion.60), channel_id=1, source_target_pairs={{0,14},{1,15},{2,12},{3,13},{4,10},{5,11},{6,8},{7,9},{8,22},{9,23... | collective-permute-start | bytes 589832 | tf_op jit(solution)/shard_map/ppermute | solution.py:27
  64.0 4.6 %collective-permute-done.13.refs_2_ = f32[384,128]{1,0:T(8,128)S(1)} collective-permute-done((f32[384,128]{1,0:T(8,128)S(1)}, f32[384,128]{1,0:T(8,128)S(1)}, u32[]{:S(2)}, u32[]{:S(2)}) %collective-permute-start.13) | collective-permute-done | bytes 196640 | tf_op jit(solution)/shard_map/ppermute | solution.py:27
  68.6 1.9 %collective-permute-start.19 = (f32[384,128]{1,0:T(8,128)S(1)}, f32[384,128]{1,0:T(8,128)S(1)}, u32[]{:S(2)}, u32[]{:S(2)}) collective-permute-start(f32[384,128]{1,0:T(8,128)S(1)} %collective-permute-done.13.refs_2_), channel_id=1, source_target_pairs={{0,2},{1,3},{2,0},{3,1},{4,6},{5,7},{6,4},{7,5},{8,10},{9,11},{10,... | collective-permute-start | bytes 589832 | tf_op jit(solution)/shard_map/ppermute | solution.py:16
  79.9 2.4 %collective-permute-start.24 = (f32[384,128]{1,0:T(8,128)S(1)}, f32[384,128]{1,0:T(8,128)S(1)}, u32[]{:S(2)}, u32[]{:S(2)}) collective-permute-start(f32[384,128]{1,0:T(8,128)S(1)} %parent_rows.8), channel_id=1, source_target_pairs={{0,2},{1,3},{2,0},{3,1},{4,6},{5,7},{6,4},{7,5},{8,10},{9,11},{10,... | collective-permute-start | bytes 589832 | tf_op jit(solution)/shard_map/ppermute | solution.py:16
  83.0 3.8 %collective-permute-start.22 = (f32[512,128]{1,0:T(8,128)S(1)}, f32[512,128]{1,0:T(8,128)S(1)}, u32[]{:S(2)}, u32[]{:S(2)}) collective-permute-start(f32[512,128]{1,0:T(8,128)S(1)} %slice.58), channel_id=1, source_target_pairs={{0,8},{8,16},{16,24},{1,9},{9,17},{17,25},{2,10},{10,18},{18,26},{... | collective-permute-start | bytes 786440 | tf_op jit(solution)/shard_map/ppermute | solution.py:274
  90.1 2.2 %collective-permute-done.22 = f32[512,128]{1,0:T(8,128)S(1)} collective-permute-done((f32[512,128]{1,0:T(8,128)S(1)}, f32[512,128]{1,0:T(8,128)S(1)}, u32[]{:S(2)}, u32[]{:S(2)}) %collective-permute-start.22) | collective-permute-done | bytes 262176 | tf_op jit(solution)/shard_map/ppermute | solution.py:274
  96.1 2.5 %collective-permute-done.23 = f32[384,128]{1,0:T(8,128)S(1)} collective-permute-done((f32[384,128]{1,0:T(8,128)S(1)}, f32[384,128]{1,0:T(8,128)S(1)}, u32[]{:S(2)}, u32[]{:S(2)}) %collective-permute-start.23) | collective-permute-done | bytes 196640 | tf_op jit(solution)/shard_map/ppermute | solution.py:16
  99.0 4.2 %collective-permute-start.26 = (f32[384,128]{1,0:T(8,128)S(1)}, f32[384,128]{1,0:T(8,128)S(1)}, u32[]{:S(2)}, u32[]{:S(2)}) collective-permute-start(f32[384,128]{1,0:T(8,128)S(1)} %fusion.59), channel_id=1, source_target_pairs={{0,14},{1,15},{2,12},{3,13},{4,10},{5,11},{6,8},{7,9},{8,22},{9,23... | collective-permute-start | bytes 589832 | tf_op jit(solution)/shard_map/ppermute | solution.py:27
  104.8 5.7 %collective-permute-done.26.refs_2_ = f32[384,128]{1,0:T(8,128)S(1)} collective-permute-done((f32[384,128]{1,0:T(8,128)S(1)}, f32[384,128]{1,0:T(8,128)S(1)}, u32[]{:S(2)}, u32[]{:S(2)}) %collective-permute-start.26) | collective-permute-done | bytes 196640 | tf_op jit(solution)/shard_map/ppermute | solution.py:27
  112.9 4.1 %collective-permute-done.27.refs_0_ = f32[384,128]{1,0:T(8,128)S(1)} collective-permute-done((f32[384,128]{1,0:T(8,128)S(1)}, f32[384,128]{1,0:T(8,128)S(1)}, u32[]{:S(2)}, u32[]{:S(2)}) %collective-permute-start.27) | collective-permute-done | bytes 196640 | tf_op jit(solution)/shard_map/ppermute | solution.py:27
  124.7 4.3 %collective-permute-start.35 = (f32[512,128]{1,0:T(8,128)S(1)}, f32[512,128]{1,0:T(8,128)S(1)}, u32[]{:S(2)}, u32[]{:S(2)}) collective-permute-start(f32[512,128]{1,0:T(8,128)S(1)} %slice.62), channel_id=1, source_target_pairs={{0,8},{8,16},{16,24},{1,9},{9,17},{17,25},{2,10},{10,18},{18,26},{... | collective-permute-start | bytes 786440 | tf_op jit(solution)/shard_map/ppermute | solution.py:274
  131.2 5.6 %collective-permute-done.37 = f32[384,128]{1,0:T(8,128)S(1)} collective-permute-done((f32[384,128]{1,0:T(8,128)S(1)}, f32[384,128]{1,0:T(8,128)S(1)}, u32[]{:S(2)}, u32[]{:S(2)}) %collective-permute-start.37) | collective-permute-done | bytes 196640 | tf_op jit(solution)/shard_map/ppermute | solution.py:16
  140.7 3.9 %collective-permute-done.36 = f32[384,128]{1,0:T(8,128)S(1)} collective-permute-done((f32[384,128]{1,0:T(8,128)S(1)}, f32[384,128]{1,0:T(8,128)S(1)}, u32[]{:S(2)}, u32[]{:S(2)}) %collective-permute-start.36) | collective-permute-done | bytes 196640 | tf_op jit(solution)/shard_map/ppermute | solution.py:16
  (135 shorter events, 61.8 us)
Async XLA Ops:
  6.4 19.9 %collective-permute-start.3 = (f32[384,128]{1,0:T(8,128)}, f32[384,128]{1,0:T(8,128)}, u32[]{:S(2)}, u32[]{:S(2)}) collective-permute-start(f32[384,128]{1,0:T(8,128)} %fusion.46.refs_0_), channel_id=1, source_target_pairs={{0,2},{1,3},{2,0},{3,1},{4,6},{5,7},{6,4},{7,5},{8,10},{9,11},{10,... | collective-permute-start | bytes 589832 | tf_op jit(solution)/shard_map/ppermute | solution.py:16
  9.5 11.7 %collective-permute-start.1 = (f32[384,128]{1,0:T(8,128)}, f32[384,128]{1,0:T(8,128)}, u32[]{:S(2)}, u32[]{:S(2)}) collective-permute-start(f32[384,128]{1,0:T(8,128)} %fusion.46.refs_0_), channel_id=1, source_target_pairs={{0,6},{1,7},{2,4},{3,5},{4,2},{5,3},{6,0},{7,1},{8,14},{9,15},{10,... | collective-permute-start | bytes 589832 | tf_op jit(solution)/shard_map/ppermute | solution.py:16
  12.0 16.6 %collective-permute-start = (f32[384,128]{1,0:T(8,128)}, f32[384,128]{1,0:T(8,128)}, u32[]{:S(2)}, u32[]{:S(2)}) collective-permute-start(f32[384,128]{1,0:T(8,128)} %fusion.46.refs_0_), channel_id=1, source_target_pairs={{0,1},{1,0},{2,3},{3,2},{4,5},{5,4},{6,7},{7,6},{8,9},{9,8},{10,11... | collective-permute-start | bytes 589832 | tf_op jit(solution)/shard_map/ppermute | solution.py:16
  21.2 6.0 %collective-permute-start.5 = (f32[384,128]{1,0:T(8,128)}, f32[384,128]{1,0:T(8,128)}, u32[]{:S(2)}, u32[]{:S(2)}) collective-permute-start(f32[384,128]{1,0:T(8,128)} %collective-permute-done.1.refs_2_), channel_id=1, source_target_pairs={{0,2},{1,3},{2,0},{3,1},{4,6},{5,7},{6,4},{7,5},{8,10},{9,11},{10,... | collective-permute-start | bytes 589832 | tf_op jit(solution)/shard_map/ppermute | solution.py:16
  23.9 20.5 %collective-permute-start.12 = (f32[384,512]{1,0:T(8,128)}, f32[384,512]{1,0:T(8,128)}, u32[]{:S(2)}, u32[]{:S(2)}) collective-permute-start(f32[384,512]{1,0:T(8,128)} %fusion.20), channel_id=1, source_target_pairs={{0,24},{1,25},{2,26},{3,27},{4,28},{5,29},{6,30},{7,31},{8,0},{9,1... | collective-permute-start | bytes 2359304 | tf_op jit(solution)/shard_map/ppermute | solution.py:27
  36.7 20.0 %collective-permute-start.11 = (f32[384,256]{1,0:T(8,128)S(1)}, f32[384,256]{1,0:T(8,128)S(1)}, u32[]{:S(2)}, u32[]{:S(2)}) collective-permute-start(f32[384,256]{1,0:T(8,128)S(1)} %fusion.52), channel_id=1, source_target_pairs={{0,24},{1,25},{2,26},{3,27},{4,28},{5,29},{6,30},{7,31},{8,0},{9,1... | collective-permute-start | bytes 1179656 | tf_op jit(solution)/shard_map/ppermute | solution.py:27
  40.6 8.4 %collective-permute-start.9 = (f32[384,128]{1,0:T(8,128)S(1)}, f32[384,128]{1,0:T(8,128)S(1)}, u32[]{:S(2)}, u32[]{:S(2)}) collective-permute-start(f32[384,128]{1,0:T(8,128)S(1)} %parent_rows.6), channel_id=1, source_target_pairs={{0,2},{1,3},{2,0},{3,1},{4,6},{5,7},{6,4},{7,5},{8,10},{9,11},{10,... | collective-permute-start | bytes 589832 | tf_op jit(solution)/shard_map/ppermute | solution.py:16
  47.3 7.2 %collective-permute-start.8 = (f32[384,128]{1,0:T(8,128)S(1)}, f32[384,128]{1,0:T(8,128)S(1)}, u32[]{:S(2)}, u32[]{:S(2)}) collective-permute-start(f32[384,128]{1,0:T(8,128)S(1)} %get-tuple-element.20), channel_id=1, source_target_pairs={{0,2},{1,3},{2,0},{3,1},{4,6},{5,7},{6,4},{7,5},{8,10},{9,11},{10,... | collective-permute-start | bytes 589832 | tf_op jit(solution)/shard_map/ppermute | solution.py:16
  49.1 7.6 %collective-permute-start.10 = (f32[384,128]{1,0:T(8,128)S(1)}, f32[384,128]{1,0:T(8,128)S(1)}, u32[]{:S(2)}, u32[]{:S(2)}) collective-permute-start(f32[384,128]{1,0:T(8,128)S(1)} %add.51), channel_id=1, source_target_pairs={{0,6},{1,7},{2,4},{3,5},{4,2},{5,3},{6,0},{7,1},{8,14},{9,15},{10,... | collective-permute-start | bytes 589832 | tf_op jit(solution)/shard_map/ppermute | solution.py:16
  57.2 11.4 %collective-permute-start.13 = (f32[384,128]{1,0:T(8,128)S(1)}, f32[384,128]{1,0:T(8,128)S(1)}, u32[]{:S(2)}, u32[]{:S(2)}) collective-permute-start(f32[384,128]{1,0:T(8,128)S(1)} %fusion.60), channel_id=1, source_target_pairs={{0,14},{1,15},{2,12},{3,13},{4,10},{5,11},{6,8},{7,9},{8,22},{9,23... | collective-permute-start | bytes 589832 | tf_op jit(solution)/shard_map/ppermute | solution.py:27
  62.2 9.9 %collective-permute-start.17 = (f32[384,128]{1,0:T(8,128)S(1)}, f32[384,128]{1,0:T(8,128)S(1)}, u32[]{:S(2)}, u32[]{:S(2)}) collective-permute-start(f32[384,128]{1,0:T(8,128)S(1)} %fusion.60), channel_id=1, source_target_pairs={{0,10},{1,11},{2,8},{3,9},{4,14},{5,15},{6,12},{7,13},{8,18},{9,19... | collective-permute-start | bytes 589832 | tf_op jit(solution)/shard_map/ppermute | solution.py:27
  62.3 9.9 %collective-permute-start.14 = (f32[384,128]{1,0:T(8,128)S(1)}, f32[384,128]{1,0:T(8,128)S(1)}, u32[]{:S(2)}, u32[]{:S(2)}) collective-permute-start(f32[384,128]{1,0:T(8,128)S(1)} %fusion.60), channel_id=1, source_target_pairs={{0,8},{1,9},{2,10},{3,11},{4,12},{5,13},{6,14},{7,15},{8,16},{9,17... | collective-permute-start | bytes 589832 | tf_op jit(solution)/shard_map/ppermute | solution.py:27
  79.9 8.4 %collective-permute-start.24 = (f32[384,128]{1,0:T(8,128)S(1)}, f32[384,128]{1,0:T(8,128)S(1)}, u32[]{:S(2)}, u32[]{:S(2)}) collective-permute-start(f32[384,128]{1,0:T(8,128)S(1)} %parent_rows.8), channel_id=1, source_target_pairs={{0,2},{1,3},{2,0},{3,1},{4,6},{5,7},{6,4},{7,5},{8,10},{9,11},{10,... | collective-permute-start | bytes 589832 | tf_op jit(solution)/shard_map/ppermute | solution.py:16
  83.0 9.3 %collective-permute-start.22 = (f32[512,128]{1,0:T(8,128)S(1)}, f32[512,128]{1,0:T(8,128)S(1)}, u32[]{:S(2)}, u32[]{:S(2)}) collective-permute-start(f32[512,128]{1,0:T(8,128)S(1)} %slice.58), channel_id=1, source_target_pairs={{0,8},{8,16},{16,24},{1,9},{9,17},{17,25},{2,10},{10,18},{18,26},{... | collective-permute-start | bytes 786440 | tf_op jit(solution)/shard_map/ppermute | solution.py:274
  87.9 10.7 %collective-permute-start.23 = (f32[384,128]{1,0:T(8,128)S(1)}, f32[384,128]{1,0:T(8,128)S(1)}, u32[]{:S(2)}, u32[]{:S(2)}) collective-permute-start(f32[384,128]{1,0:T(8,128)S(1)} %get-tuple-element.26), channel_id=1, source_target_pairs={{0,2},{1,3},{2,0},{3,1},{4,6},{5,7},{6,4},{7,5},{8,10},{9,11},{10,... | collective-permute-start | bytes 589832 | tf_op jit(solution)/shard_map/ppermute | solution.py:16
  88.4 10.2 %collective-permute-start.25 = (f32[384,128]{1,0:T(8,128)S(1)}, f32[384,128]{1,0:T(8,128)S(1)}, u32[]{:S(2)}, u32[]{:S(2)}) collective-permute-start(f32[384,128]{1,0:T(8,128)S(1)} %add.56), channel_id=1, source_target_pairs={{0,6},{1,7},{2,4},{3,5},{4,2},{5,3},{6,0},{7,1},{8,14},{9,15},{10,... | collective-permute-start | bytes 589832 | tf_op jit(solution)/shard_map/ppermute | solution.py:16
  99.0 11.5 %collective-permute-start.26 = (f32[384,128]{1,0:T(8,128)S(1)}, f32[384,128]{1,0:T(8,128)S(1)}, u32[]{:S(2)}, u32[]{:S(2)}) collective-permute-start(f32[384,128]{1,0:T(8,128)S(1)} %fusion.59), channel_id=1, source_target_pairs={{0,14},{1,15},{2,12},{3,13},{4,10},{5,11},{6,8},{7,9},{8,22},{9,23... | collective-permute-start | bytes 589832 | tf_op jit(solution)/shard_map/ppermute | solution.py:27
  103.2 9.8 %collective-permute-start.30 = (f32[384,128]{1,0:T(8,128)S(1)}, f32[384,128]{1,0:T(8,128)S(1)}, u32[]{:S(2)}, u32[]{:S(2)}) collective-permute-start(f32[384,128]{1,0:T(8,128)S(1)} %fusion.59), channel_id=1, source_target_pairs={{0,10},{1,11},{2,8},{3,9},{4,14},{5,15},{6,12},{7,13},{8,18},{9,19... | collective-permute-start | bytes 589832 | tf_op jit(solution)/shard_map/ppermute | solution.py:27
  103.2 13.9 %collective-permute-start.27 = (f32[384,128]{1,0:T(8,128)S(1)}, f32[384,128]{1,0:T(8,128)S(1)}, u32[]{:S(2)}, u32[]{:S(2)}) collective-permute-start(f32[384,128]{1,0:T(8,128)S(1)} %fusion.59), channel_id=1, source_target_pairs={{0,8},{1,9},{2,10},{3,11},{4,12},{5,13},{6,14},{7,15},{8,16},{9,17... | collective-permute-start | bytes 589832 | tf_op jit(solution)/shard_map/ppermute | solution.py:27
  110.5 7.1 %collective-permute-start.32 = (f32[384,128]{1,0:T(8,128)S(1)}, f32[384,128]{1,0:T(8,128)S(1)}, u32[]{:S(2)}, u32[]{:S(2)}) collective-permute-start(f32[384,128]{1,0:T(8,128)S(1)} %collective-permute-done.26.refs_2_), channel_id=1, source_target_pairs={{0,2},{1,3},{2,0},{3,1},{4,6},{5,7},{6,4},{7,5},{8,10},{9,11},{10,... | collective-permute-start | bytes 589832 | tf_op jit(solution)/shard_map/ppermute | solution.py:16
  124.7 13.8 %collective-permute-start.35 = (f32[512,128]{1,0:T(8,128)S(1)}, f32[512,128]{1,0:T(8,128)S(1)}, u32[]{:S(2)}, u32[]{:S(2)}) collective-permute-start(f32[512,128]{1,0:T(8,128)S(1)} %slice.62), channel_id=1, source_target_pairs={{0,8},{8,16},{16,24},{1,9},{9,17},{17,25},{2,10},{10,18},{18,26},{... | collective-permute-start | bytes 786440 | tf_op jit(solution)/shard_map/ppermute | solution.py:274
  129.0 7.8 %collective-permute-start.37 = (f32[384,128]{1,0:T(8,128)S(1)}, f32[384,128]{1,0:T(8,128)S(1)}, u32[]{:S(2)}, u32[]{:S(2)}) collective-permute-start(f32[384,128]{1,0:T(8,128)S(1)} %parent_rows.10), channel_id=1, source_target_pairs={{0,2},{1,3},{2,0},{3,1},{4,6},{5,7},{6,4},{7,5},{8,10},{9,11},{10,... | collective-permute-start | bytes 589832 | tf_op jit(solution)/shard_map/ppermute | solution.py:16
  129.7 14.9 %collective-permute-start.36 = (f32[384,128]{1,0:T(8,128)S(1)}, f32[384,128]{1,0:T(8,128)S(1)}, u32[]{:S(2)}, u32[]{:S(2)}) collective-permute-start(f32[384,128]{1,0:T(8,128)S(1)} %get-tuple-element.32), channel_id=1, source_target_pairs={{0,2},{1,3},{2,0},{3,1},{4,6},{5,7},{6,4},{7,5},{8,10},{9,11},{10,... | collective-permute-start | bytes 589832 | tf_op jit(solution)/shard_map/ppermute | solution.py:16
  136.8 7.7 %collective-permute-start.38 = (f32[384,128]{1,0:T(8,128)S(1)}, f32[384,128]{1,0:T(8,128)S(1)}, u32[]{:S(2)}, u32[]{:S(2)}) collective-permute-start(f32[384,128]{1,0:T(8,128)S(1)} %add.61), channel_id=1, source_target_pairs={{0,6},{1,7},{2,4},{3,5},{4,2},{5,3},{6,0},{7,1},{8,14},{9,15},{10,... | collective-permute-start | bytes 589832 | tf_op jit(solution)/shard_map/ppermute | solution.py:16
  (34 other events, 150.0 us)

commit v3 on v2

--- a/solution.py
+++ b/solution.py
@@ -130,11 +130,7 @@
         in_specs=[smem] * 3 + [vmem] * (2 + len(blocks)),
         out_specs=vmem,
         compiler_params=pltpu.CompilerParams(vmem_limit_bytes=VMEM_BYTES),
-        cost_estimate=pl.CostEstimate(
-            flops=4 * order * rows.shape[1] * columns * len(blocks),
-            bytes_accessed=8 * order * columns,
-            transcendentals=0,
-        ),
+        cost_estimate=pl.CostEstimate(flops=1000, bytes_accessed=1000, transcendentals=0),
         name="rows_subtracted",
     )(place, parents, counts, rows, sources, *blocks.values())
 
@@ -150,9 +146,7 @@
         out_specs=vmem,
         scratch_shapes=[pltpu.VMEM(partial_rhs.shape, jnp.float32)],
         compiler_params=pltpu.CompilerParams(vmem_limit_bytes=VMEM_BYTES),
-        cost_estimate=pl.CostEstimate(
-            flops=8 * order * order * columns, bytes_accessed=4 * order * (order + 256), transcendentals=0
-        ),
+        cost_estimate=pl.CostEstimate(flops=1000, bytes_accessed=1000, transcendentals=0),
         name="parent_solve",
     )(place, parents, counts, rows, high, low, partial_rhs, *blocks.values())
 
@@ -200,12 +194,42 @@
         out_specs=[vmem] * len(wanted),
         scratch_shapes=[pltpu.VMEM((2, order, 2 * columns), jnp.bfloat16)],
         compiler_params=pltpu.CompilerParams(vmem_limit_bytes=VMEM_BYTES),
-        cost_estimate=pl.CostEstimate(
-            flops=4 * cap * order * columns * len(wanted), bytes_accessed=8 * order * columns, transcendentals=0
-        ),
+        cost_estimate=pl.CostEstimate(flops=1000, bytes_accessed=1000, transcendentals=0),
         name="parent_rows",
     )(place, parents, counts, rows, own, other)
     return dict(zip(wanted, found))
+
+
+def split_product(matrix, wide, columns):
+    high = matrix.astype(jnp.bfloat16)
+    low = (matrix - high.astype(jnp.float32)).astype(jnp.bfloat16)
+    return summed(jnp.dot(high, wide, preferred_element_type=jnp.float32)) + jnp.dot(
+        low, wide[:, :columns], preferred_element_type=jnp.float32
+    )
+
+
+def last_kernel(tick, downward, partial_solution, descended, earlier, out, result, sent):
+    del earlier
+    columns = result.shape[1]
+    result[...] = partial_solution[...] - split_product(downward[...], side_by_side(descended[...]), columns)
+    copy = pltpu.make_async_copy(result, out.at[tick], sent)
+    copy.start()
+    copy.wait()
+
+
+def last_leaf(downward, partial_solution, descended, earlier, tick):
+    vmem = pl.BlockSpec(memory_space=pltpu.VMEM)
+    return pl.pallas_call(
+        functools.partial(last_kernel, tick),
+        out_shape=jax.ShapeDtypeStruct(earlier.shape, jnp.float32),
+        in_specs=[vmem] * 3 + [pl.BlockSpec(memory_space=pl.ANY)],
+        out_specs=pl.BlockSpec(memory_space=pl.ANY),
+        scratch_shapes=[pltpu.VMEM(partial_solution.shape, jnp.float32), pltpu.SemaphoreType.DMA],
+        input_output_aliases={3: 0},
+        compiler_params=pltpu.CompilerParams(vmem_limit_bytes=VMEM_BYTES),
+        cost_estimate=pl.CostEstimate(flops=1000, bytes_accessed=1000, transcendentals=0),
+        name="last_leaf",
+    )(downward, partial_solution, descended, earlier)
 
 
 def local(
@@ -241,16 +265,15 @@
     sources = leaf_sources[0, 0]
     partial_solution = product(inverse, sources[0])
     update = product(upward, partial_solution)
-    held = spread({0: update}, masks)
     parent_high, parent_low = halves(parent_inv[0, 0])
 
     later = jnp.concatenate([sources[tick] for tick in range(1, ticks)], axis=1)
     along = product(upward, inverse)
     through = jnp.where(lax.axis_index("panel") > 0, product(along, coupling), 0.0)
+    own_later = product(inverse, later)
+    held = spread({0: update}, masks)
     next_through = onward(through, -1, 0)
     next_sources = onward(product(along, later), -1, 0)
-    next_descended = product(next_through, edge(downward))
-    own_later = product(inverse, later)
 
     tables = (place, parent_of, update_count, row_ids)
     leaf_out = jnp.zeros(sources.shape, jnp.float32)
@@ -266,28 +289,31 @@
         solved = parent_solve(*tables, parent_high, parent_low, partial_rhs, late)
         other = swapped(solved, TWIN)
         parts = parent_rows(*tables, solved, other, span[-1:])
-        parts.update(parent_rows(*tables, after(solved, parts[span[-1]]), other, span[:-1]))
+        first = (parts[span[-1]], own_later) if tick == 0 else parts[span[-1]]
+        parts.update(parent_rows(*tables, after(solved, first), other, span[:-1]))
         descended = delivered(parts, masks)
+        if tick == 0:
+            next_through = after(next_through, parts[0])
+            next_descended = product(next_through, edge(downward))
         at = slice((tick - 1) * columns, tick * columns)
         if tick > 0:
-            leaving = after(edge(leaf_now), parts[0])
+            leaving = after(edge(leaf_now), parts[span[-1]])
             interface = lax.ppermute(leaving, "panel", [(spot, spot + 1) for spot in range(panels - 1)])
             partial_solution = own_later[:, at] + product(inverse, product(coupling, interface))
         if tick + 1 < ticks:
             at = slice(tick * columns, (tick + 1) * columns)
             base = next_sources[:, at] + product(next_through, edge(partial_solution))
             update = base - product(next_descended, descended)
-            moved = {offset: onward(update, 1, offset) for offset in masks}
-            moved[0] = onward(update, 1, 0)
+            moved = {offset: onward(update, 1, offset) for offset in (*masks, 0)}
             held = dict(moved)
             for step, mask in enumerate(masks):
                 for offset in offsets(masks[:step]):
                     if offset ^ mask not in held:
                         held[offset ^ mask] = swapped(held[offset], mask)
             leaf_now = partial_solution - product(downward, after(descended, moved[masks[0]]))
+            leaf_out = lax.dynamic_update_index_in_dim(leaf_out, leaf_now, tick, 0)
         else:
-            leaf_now = partial_solution - product(downward, descended)
-        leaf_out = lax.dynamic_update_index_in_dim(leaf_out, leaf_now, tick, 0)
+            leaf_out = last_leaf(downward, partial_solution, descended, leaf_out, tick)
         parent_out = lax.dynamic_update_index_in_dim(parent_out, solved, tick, 0)
     return (leaf_out[None, None], parent_out[None, None])
 

time: 149 us -> 143 us (0.960)
  local copies, waits for them, and re-layouts: 6.8 us -> 2.02 us
  waiting for transfers between devices: 52.5 us -> 48.6 us
  Pallas kernels: 13.9 us -> 16 us
    ppermute x8, waiting for transfers between devices: 21.1 us -> 14.4 us  [onward(): return lax.ppermute(value, ('panel', 'front'), pairs)]
    ppermute x29, waiting for transfers between devices: 29.1 us -> 34.2 us  [swapped(): lax.ppermute(value, 'front', [(place, place ^ mask) for place in range(co...]
    ppermute x2, starting transfers between devices: 8.02 us -> 3.03 us  [local(): lax.ppermute(leaving, 'panel', [(spot, spot + 1) for spot in range(panels...]
    unnamed x38 -> x24, local copies, waits for them, and re-layouts: 6.5 us -> 1.72 us
    ppermute x29, starting transfers between devices: 22.9 us -> 25.4 us  [swapped(): lax.ppermute(value, 'front', [(place, place ^ mask) for place in range(co...]
    pallas_call x6, Pallas kernels: 4.26 us -> 6.6 us  [parent_rows(): pl.pallas_call(functools.partial(rows_kernel, wanted), out_shape=[jax.Sha...]
    ppermute x2, waiting for transfers between devices: 2.23 us -> 0.01 us  [local(): lax.ppermute(leaving, 'panel', [(spot, spot + 1) for spot in range(panels...]
    pallas_call x3, Pallas kernels: 3.85 us -> 1.89 us  [rows_subtracted(): pl.pallas_call(functools.partial(early_kernel, list(blocks), tick), out_s...]
  transfers between devices with their start and end apart: 39 -> 39, of which waited for: 21 -> 22; matrix products, arithmetic and copies ran while one was open for 12% -> 15% of each run, Pallas kernels for 6% -> 6%
where the time goes in v3:
time: 143 us; the launch traced here: 141 us
  waiting for transfers between devices  48.6 us (34%)
  starting transfers between devices  48.4 us (34%)
  matrix products  22.5 us (16%)
  Pallas kernels  16 us (11%)
  other arithmetic  2.18 us (2%)
  local copies, waits for them, and re-layouts  2.02 us (1%)
    ppermute x29, waiting for transfers between devices, swapped(): lax.ppermute(value, 'front', [(place, place ^ mask) for place in range(co...  34.2 us
    ppermute x29, starting transfers between devices, swapped(): lax.ppermute(value, 'front', [(place, place ^ mask) for place in range(co...  25.4 us
    dot_general x17, matrix products, product(): jnp.dot(matrix, operand, precision=lax.Precision.HIGH, preferred_element_...  22.5 us
    ppermute x8, starting transfers between devices, onward(): return lax.ppermute(value, ('panel', 'front'), pairs)  20 us
    ppermute x8, waiting for transfers between devices, onward(): return lax.ppermute(value, ('panel', 'front'), pairs)  14.4 us
    pallas_call x6, Pallas kernels, parent_rows(): pl.pallas_call(functools.partial(rows_kernel, wanted), out_shape=[jax.Sha...  6.6 us
    pallas_call x3, Pallas kernels, parent_solve(): pl.pallas_call(functools.partial(solve_kernel, list(blocks)), out_shape=j...  6.26 us
    ppermute x2, starting transfers between devices, local(): lax.ppermute(leaving, 'panel', [(spot, spot + 1) for spot in range(panels...  3.03 us
  transfers between devices with their start and end apart: 39, of which 22 were waited for; matrix products, arithmetic and copies ran while one was open for 15% of the time, Pallas kernels for 6%

profile of v3, /device:TPU:0, one launch (start us, length us, event | category | flops | bytes accessed | tf_op | source)
XLA Modules:
  0.0 141.0 jit_solution(15901596726511466661)
XLA Ops:
  5.0 3.1 %collective-permute-start.3 = (f32[384,128]{1,0:T(8,128)S(1)}, f32[384,128]{1,0:T(8,128)S(1)}, u32[]{:S(2)}, u32[]{:S(2)}) collective-permute-start(f32[384,128]{1,0:T(8,128)S(1)} %fusion.40.refs_0_), channel_id=1, source_target_pairs={{0,2},{1,3},{2,0},{3,1},{4,6},{5,7},{6,4},{7,5},{8,10},{9,11},{10,... | collective-permute-start | bytes 589832 | tf_op jit(solution)/shard_map/ppermute | solution.py:16
  8.1 2.5 %collective-permute-start.1 = (f32[384,128]{1,0:T(8,128)S(1)}, f32[384,128]{1,0:T(8,128)S(1)}, u32[]{:S(2)}, u32[]{:S(2)}) collective-permute-start(f32[384,128]{1,0:T(8,128)S(1)} %fusion.40.refs_0_), channel_id=1, source_target_pairs={{0,6},{1,7},{2,4},{3,5},{4,2},{5,3},{6,0},{7,1},{8,14},{9,15},{10,... | collective-permute-start | bytes 589832 | tf_op jit(solution)/shard_map/ppermute | solution.py:16
  10.6 2.8 %fusion.5 = f32[384,768]{1,0:T(8,128)} fusion(f32[1,1,768,768]{3,2,1,0:T(8,128)S(1)} %copy-done, f32[1,1,384,768]{3,2,1,0:T(8,128)S(1)} %copy-done.8), kind=kOutput, calls=%fused_computation.7 | convolution fusion | flops 1358954496 | bytes 4718592 | tf_op jit(solution)/shard_map/dot_general | solution.py:64
  13.4 3.8 %fusion.20 = f32[384,512]{1,0:T(8,128)} fusion(f32[384,768]{1,0:T(8,128)} %fusion.5, f32[1,1,768,512]{3,2,1,0:T(8,128)} %param.14, pred[]{:T(512)S(6)} %gt.3), kind=kOutput, calls=%fused_computation.20 | convolution fusion | flops 906166272 | bytes 3538945 | tf_op jit(solution)/shard_map/dot_general | solution.py:64
  17.2 2.4 %collective-permute-start.12 = (f32[384,512]{1,0:T(8,128)}, f32[384,512]{1,0:T(8,128)}, u32[]{:S(2)}, u32[]{:S(2)}) collective-permute-start(f32[384,512]{1,0:T(8,128)} %fusion.20), channel_id=1, source_target_pairs={{0,24},{1,25},{2,26},{3,27},{4,28},{5,29},{6,30},{7,31},{8,0},{9,1... | collective-permute-start | bytes 2359304 | tf_op jit(solution)/shard_map/ppermute | solution.py:27
  22.9 3.7 %collective-permute-done.5.refs_0_ = f32[384,128]{1,0:T(8,128)S(1)} collective-permute-done((f32[384,128]{1,0:T(8,128)S(1)}, f32[384,128]{1,0:T(8,128)S(1)}, u32[]{:S(2)}, u32[]{:S(2)}) %collective-permute-start.5) | collective-permute-done | bytes 196640 | tf_op jit(solution)/shard_map/ppermute | solution.py:16
  28.1 2.1 %parent_solve.3.own = f32[768,128]{1,0:T(8,128)S(1)} custom-call(s32[1]{0:T(128)} %bitcast.6.place, s32[1,8]{1,0:T(1,128)S(1)} %copy-done.4, s32[1,8]{1,0:T(1,128)S(1)} %copy-done.5, s32[8,384]{1,0:T(8,128)S(1)} %bitcast.113, bf16[768,768]{1,0:T(8,128)(2,1)S(1)} %get-tuple-element.37.high, bf16[768,768]{1,0:T(8,128)(2,1)S(1)} %get-tuple-element.36.low, ...), custom_call_target="tpu_custom_call" | custom-call | flops 1000 | bytes 1000 | tf_op jit(solution)/shard_map/parent_solve/pallas_call | solution.py:142
  35.5 2.3 %collective-permute-done.12 = f32[384,512]{1,0:T(8,128)} collective-permute-done((f32[384,512]{1,0:T(8,128)}, f32[384,512]{1,0:T(8,128)}, u32[]{:S(2)}, u32[]{:S(2)}) %collective-permute-start.12) | collective-permute-done | bytes 786464 | tf_op jit(solution)/shard_map/ppermute | solution.py:27
  45.5 4.5 %collective-permute-done.10 = f32[384,128]{1,0:T(8,128)S(1)} collective-permute-done((f32[384,128]{1,0:T(8,128)S(1)}, f32[384,128]{1,0:T(8,128)S(1)}, u32[]{:S(2)}, u32[]{:S(2)}) %collective-permute-start.10) | collective-permute-done | bytes 196640 | tf_op jit(solution)/shard_map/ppermute | solution.py:16
  50.4 2.6 %collective-permute-start.13 = (f32[384,128]{1,0:T(8,128)S(1)}, f32[384,128]{1,0:T(8,128)S(1)}, u32[]{:S(2)}, u32[]{:S(2)}) collective-permute-start(f32[384,128]{1,0:T(8,128)S(1)} %fusion.54), channel_id=1, source_target_pairs={{0,14},{1,15},{2,12},{3,13},{4,10},{5,11},{6,8},{7,9},{8,22},{9,23... | collective-permute-start | bytes 589832 | tf_op jit(solution)/shard_map/ppermute | solution.py:27
  54.8 2.4 %collective-permute-start.14 = (f32[384,128]{1,0:T(8,128)S(1)}, f32[384,128]{1,0:T(8,128)S(1)}, u32[]{:S(2)}, u32[]{:S(2)}) collective-permute-start(f32[384,128]{1,0:T(8,128)S(1)} %fusion.54), channel_id=1, source_target_pairs={{0,8},{1,9},{2,10},{3,11},{4,12},{5,13},{6,14},{7,15},{8,16},{9,17... | collective-permute-start | bytes 589832 | tf_op jit(solution)/shard_map/ppermute | solution.py:27
  57.2 4.2 %collective-permute-done.13.refs_2_ = f32[384,128]{1,0:T(8,128)S(1)} collective-permute-done((f32[384,128]{1,0:T(8,128)S(1)}, f32[384,128]{1,0:T(8,128)S(1)}, u32[]{:S(2)}, u32[]{:S(2)}) %collective-permute-start.13) | collective-permute-done | bytes 196640 | tf_op jit(solution)/shard_map/ppermute | solution.py:27
  61.3 4.4 %collective-permute-start.19 = (f32[384,128]{1,0:T(8,128)S(1)}, f32[384,128]{1,0:T(8,128)S(1)}, u32[]{:S(2)}, u32[]{:S(2)}) collective-permute-start(f32[384,128]{1,0:T(8,128)S(1)} %collective-permute-done.13.refs_2_), channel_id=1, source_target_pairs={{0,2},{1,3},{2,0},{3,1},{4,6},{5,7},{6,4},{7,5},{8,10},{9,11},{10,... | collective-permute-start | bytes 589832 | tf_op jit(solution)/shard_map/ppermute | solution.py:16
  65.7 2.2 %collective-permute-done.14.refs_0_ = f32[384,128]{1,0:T(8,128)S(1)} collective-permute-done((f32[384,128]{1,0:T(8,128)S(1)}, f32[384,128]{1,0:T(8,128)S(1)}, u32[]{:S(2)}, u32[]{:S(2)}) %collective-permute-start.14) | collective-permute-done | bytes 196640 | tf_op jit(solution)/shard_map/ppermute | solution.py:27
  80.0 4.9 %collective-permute-done.24 = f32[384,128]{1,0:T(8,128)S(1)} collective-permute-done((f32[384,128]{1,0:T(8,128)S(1)}, f32[384,128]{1,0:T(8,128)S(1)}, u32[]{:S(2)}, u32[]{:S(2)}) %collective-permute-start.24) | collective-permute-done | bytes 196640 | tf_op jit(solution)/shard_map/ppermute | solution.py:16
  85.0 3.7 %collective-permute-start.25 = (f32[384,128]{1,0:T(8,128)S(1)}, f32[384,128]{1,0:T(8,128)S(1)}, u32[]{:S(2)}, u32[]{:S(2)}) collective-permute-start(f32[384,128]{1,0:T(8,128)S(1)} %add.55), channel_id=1, source_target_pairs={{0,6},{1,7},{2,4},{3,5},{4,2},{5,3},{6,0},{7,1},{8,14},{9,15},{10,... | collective-permute-start | bytes 589832 | tf_op jit(solution)/shard_map/ppermute | solution.py:16
  92.5 3.1 %collective-permute-done.25 = f32[384,128]{1,0:T(8,128)S(1)} collective-permute-done((f32[384,128]{1,0:T(8,128)S(1)}, f32[384,128]{1,0:T(8,128)S(1)}, u32[]{:S(2)}, u32[]{:S(2)}) %collective-permute-start.25) | collective-permute-done | bytes 196640 | tf_op jit(solution)/shard_map/ppermute | solution.py:16
  96.0 4.2 %collective-permute-start.26 = (f32[384,128]{1,0:T(8,128)S(1)}, f32[384,128]{1,0:T(8,128)S(1)}, u32[]{:S(2)}, u32[]{:S(2)}) collective-permute-start(f32[384,128]{1,0:T(8,128)S(1)} %fusion.53), channel_id=1, source_target_pairs={{0,14},{1,15},{2,12},{3,13},{4,10},{5,11},{6,8},{7,9},{8,22},{9,23... | collective-permute-start | bytes 589832 | tf_op jit(solution)/shard_map/ppermute | solution.py:27
  100.2 4.1 %collective-permute-start.30 = (f32[384,128]{1,0:T(8,128)S(1)}, f32[384,128]{1,0:T(8,128)S(1)}, u32[]{:S(2)}, u32[]{:S(2)}) collective-permute-start(f32[384,128]{1,0:T(8,128)S(1)} %fusion.53), channel_id=1, source_target_pairs={{0,10},{1,11},{2,8},{3,9},{4,14},{5,15},{6,12},{7,13},{8,18},{9,19... | collective-permute-start | bytes 589832 | tf_op jit(solution)/shard_map/ppermute | solution.py:27
  107.5 2.7 %collective-permute-start.32 = (f32[384,128]{1,0:T(8,128)S(1)}, f32[384,128]{1,0:T(8,128)S(1)}, u32[]{:S(2)}, u32[]{:S(2)}) collective-permute-start(f32[384,128]{1,0:T(8,128)S(1)} %collective-permute-done.26.refs_2_), channel_id=1, source_target_pairs={{0,2},{1,3},{2,0},{3,1},{4,6},{5,7},{6,4},{7,5},{8,10},{9,11},{10,... | collective-permute-start | bytes 589832 | tf_op jit(solution)/shard_map/ppermute | solution.py:16
  110.8 3.7 %collective-permute-done.27.refs_0_ = f32[384,128]{1,0:T(8,128)S(1)} collective-permute-done((f32[384,128]{1,0:T(8,128)S(1)}, f32[384,128]{1,0:T(8,128)S(1)}, u32[]{:S(2)}, u32[]{:S(2)}) %collective-permute-start.27) | collective-permute-done | bytes 196640 | tf_op jit(solution)/shard_map/ppermute | solution.py:27
  116.8 2.1 %parent_solve.5.own = f32[768,128]{1,0:T(8,128)S(1)} custom-call(s32[1]{0:T(128)} %bitcast.6.place, s32[1,8]{1,0:T(1,128)S(1)} %copy-done.4, s32[1,8]{1,0:T(1,128)S(1)} %copy-done.5, s32[8,384]{1,0:T(8,128)S(1)} %bitcast.121, bf16[768,768]{1,0:T(8,128)(2,1)S(1)} %get-tuple-element.37.high, bf16[768,768]{1,0:T(8,128)(2,1)S(1)} %get-tuple-element.36.low, ...), custom_call_target="tpu_custom_call" | custom-call | flops 1000 | bytes 1000 | tf_op jit(solution)/shard_map/parent_solve/pallas_call | solution.py:142
  126.5 4.9 %collective-permute-done.37 = f32[384,128]{1,0:T(8,128)S(1)} collective-permute-done((f32[384,128]{1,0:T(8,128)S(1)}, f32[384,128]{1,0:T(8,128)S(1)}, u32[]{:S(2)}, u32[]{:S(2)}) %collective-permute-start.37) | collective-permute-done | bytes 196640 | tf_op jit(solution)/shard_map/ppermute | solution.py:16
  134.8 4.7 %collective-permute-done.38 = f32[384,128]{1,0:T(8,128)S(1)} collective-permute-done((f32[384,128]{1,0:T(8,128)S(1)}, f32[384,128]{1,0:T(8,128)S(1)}, u32[]{:S(2)}, u32[]{:S(2)}) %collective-permute-start.38) | collective-permute-done | bytes 196640 | tf_op jit(solution)/shard_map/ppermute | solution.py:16
  (122 shorter events, 58.6 us)
Async XLA Ops:
  5.0 17.4 %collective-permute-start.3 = (f32[384,128]{1,0:T(8,128)S(1)}, f32[384,128]{1,0:T(8,128)S(1)}, u32[]{:S(2)}, u32[]{:S(2)}) collective-permute-start(f32[384,128]{1,0:T(8,128)S(1)} %fusion.40.refs_0_), channel_id=1, source_target_pairs={{0,2},{1,3},{2,0},{3,1},{4,6},{5,7},{6,4},{7,5},{8,10},{9,11},{10,... | collective-permute-start | bytes 589832 | tf_op jit(solution)/shard_map/ppermute | solution.py:16
  8.1 11.5 %collective-permute-start.1 = (f32[384,128]{1,0:T(8,128)S(1)}, f32[384,128]{1,0:T(8,128)S(1)}, u32[]{:S(2)}, u32[]{:S(2)}) collective-permute-start(f32[384,128]{1,0:T(8,128)S(1)} %fusion.40.refs_0_), channel_id=1, source_target_pairs={{0,6},{1,7},{2,4},{3,5},{4,2},{5,3},{6,0},{7,1},{8,14},{9,15},{10,... | collective-permute-start | bytes 589832 | tf_op jit(solution)/shard_map/ppermute | solution.py:16
  10.6 16.1 %collective-permute-start = (f32[384,128]{1,0:T(8,128)S(1)}, f32[384,128]{1,0:T(8,128)S(1)}, u32[]{:S(2)}, u32[]{:S(2)}) collective-permute-start(f32[384,128]{1,0:T(8,128)S(1)} %fusion.40.refs_0_), channel_id=1, source_target_pairs={{0,1},{1,0},{2,3},{3,2},{4,5},{5,4},{6,7},{7,6},{8,9},{9,8},{10,11... | collective-permute-start | bytes 589832 | tf_op jit(solution)/shard_map/ppermute | solution.py:16
  17.2 20.7 %collective-permute-start.12 = (f32[384,512]{1,0:T(8,128)}, f32[384,512]{1,0:T(8,128)}, u32[]{:S(2)}, u32[]{:S(2)}) collective-permute-start(f32[384,512]{1,0:T(8,128)} %fusion.20), channel_id=1, source_target_pairs={{0,24},{1,25},{2,26},{3,27},{4,28},{5,29},{6,30},{7,31},{8,0},{9,1... | collective-permute-start | bytes 2359304 | tf_op jit(solution)/shard_map/ppermute | solution.py:27
  31.0 19.1 %collective-permute-start.11 = (f32[384,256]{1,0:T(8,128)S(1)}, f32[384,256]{1,0:T(8,128)S(1)}, u32[]{:S(2)}, u32[]{:S(2)}) collective-permute-start(f32[384,256]{1,0:T(8,128)S(1)} %fusion.46), channel_id=1, source_target_pairs={{0,24},{1,25},{2,26},{3,27},{4,28},{5,29},{6,30},{7,31},{8,0},{9,1... | collective-permute-start | bytes 1179656 | tf_op jit(solution)/shard_map/ppermute | solution.py:27
  33.9 7.8 %collective-permute-start.9 = (f32[384,128]{1,0:T(8,128)S(1)}, f32[384,128]{1,0:T(8,128)S(1)}, u32[]{:S(2)}, u32[]{:S(2)}) collective-permute-start(f32[384,128]{1,0:T(8,128)S(1)} %parent_rows.6), channel_id=1, source_target_pairs={{0,2},{1,3},{2,0},{3,1},{4,6},{5,7},{6,4},{7,5},{8,10},{9,11},{10,... | collective-permute-start | bytes 589832 | tf_op jit(solution)/shard_map/ppermute | solution.py:16
  37.8 7.6 %collective-permute-start.8 = (f32[384,128]{1,0:T(8,128)S(1)}, f32[384,128]{1,0:T(8,128)S(1)}, u32[]{:S(2)}, u32[]{:S(2)}) collective-permute-start(f32[384,128]{1,0:T(8,128)S(1)} %get-tuple-element.21), channel_id=1, source_target_pairs={{0,2},{1,3},{2,0},{3,1},{4,6},{5,7},{6,4},{7,5},{8,10},{9,11},{10,... | collective-permute-start | bytes 589832 | tf_op jit(solution)/shard_map/ppermute | solution.py:16
  41.7 8.3 %collective-permute-start.10 = (f32[384,128]{1,0:T(8,128)S(1)}, f32[384,128]{1,0:T(8,128)S(1)}, u32[]{:S(2)}, u32[]{:S(2)}) collective-permute-start(f32[384,128]{1,0:T(8,128)S(1)} %add.50), channel_id=1, source_target_pairs={{0,6},{1,7},{2,4},{3,5},{4,2},{5,3},{6,0},{7,1},{8,14},{9,15},{10,... | collective-permute-start | bytes 589832 | tf_op jit(solution)/shard_map/ppermute | solution.py:16
  50.4 10.9 %collective-permute-start.13 = (f32[384,128]{1,0:T(8,128)S(1)}, f32[384,128]{1,0:T(8,128)S(1)}, u32[]{:S(2)}, u32[]{:S(2)}) collective-permute-start(f32[384,128]{1,0:T(8,128)S(1)} %fusion.54), channel_id=1, source_target_pairs={{0,14},{1,15},{2,12},{3,13},{4,10},{5,11},{6,8},{7,9},{8,22},{9,23... | collective-permute-start | bytes 589832 | tf_op jit(solution)/shard_map/ppermute | solution.py:27
  53.1 12.6 %collective-permute-start.17 = (f32[384,128]{1,0:T(8,128)S(1)}, f32[384,128]{1,0:T(8,128)S(1)}, u32[]{:S(2)}, u32[]{:S(2)}) collective-permute-start(f32[384,128]{1,0:T(8,128)S(1)} %fusion.54), channel_id=1, source_target_pairs={{0,10},{1,11},{2,8},{3,9},{4,14},{5,15},{6,12},{7,13},{8,18},{9,19... | collective-permute-start | bytes 589832 | tf_op jit(solution)/shard_map/ppermute | solution.py:27
  54.8 13.1 %collective-permute-start.14 = (f32[384,128]{1,0:T(8,128)S(1)}, f32[384,128]{1,0:T(8,128)S(1)}, u32[]{:S(2)}, u32[]{:S(2)}) collective-permute-start(f32[384,128]{1,0:T(8,128)S(1)} %fusion.54), channel_id=1, source_target_pairs={{0,8},{1,9},{2,10},{3,11},{4,12},{5,13},{6,14},{7,15},{8,16},{9,17... | collective-permute-start | bytes 589832 | tf_op jit(solution)/shard_map/ppermute | solution.py:27
  61.3 8.1 %collective-permute-start.19 = (f32[384,128]{1,0:T(8,128)S(1)}, f32[384,128]{1,0:T(8,128)S(1)}, u32[]{:S(2)}, u32[]{:S(2)}) collective-permute-start(f32[384,128]{1,0:T(8,128)S(1)} %collective-permute-done.13.refs_2_), channel_id=1, source_target_pairs={{0,2},{1,3},{2,0},{3,1},{4,6},{5,7},{6,4},{7,5},{8,10},{9,11},{10,... | collective-permute-start | bytes 589832 | tf_op jit(solution)/shard_map/ppermute | solution.py:16
  75.8 12.9 %collective-permute-start.22 = (f32[512,128]{1,0:T(8,128)S(1)}, f32[512,128]{1,0:T(8,128)S(1)}, u32[]{:S(2)}, u32[]{:S(2)}) collective-permute-start(f32[512,128]{1,0:T(8,128)S(1)} %slice.59), channel_id=1, source_target_pairs={{0,8},{8,16},{16,24},{1,9},{9,17},{17,25},{2,10},{10,18},{18,26},{... | collective-permute-start | bytes 786440 | tf_op jit(solution)/shard_map/ppermute | solution.py:301
  77.1 7.8 %collective-permute-start.24 = (f32[384,128]{1,0:T(8,128)S(1)}, f32[384,128]{1,0:T(8,128)S(1)}, u32[]{:S(2)}, u32[]{:S(2)}) collective-permute-start(f32[384,128]{1,0:T(8,128)S(1)} %parent_rows.8), channel_id=1, source_target_pairs={{0,2},{1,3},{2,0},{3,1},{4,6},{5,7},{6,4},{7,5},{8,10},{9,11},{10,... | collective-permute-start | bytes 589832 | tf_op jit(solution)/shard_map/ppermute | solution.py:16
  79.6 12.9 %collective-permute-start.23 = (f32[384,128]{1,0:T(8,128)S(1)}, f32[384,128]{1,0:T(8,128)S(1)}, u32[]{:S(2)}, u32[]{:S(2)}) collective-permute-start(f32[384,128]{1,0:T(8,128)S(1)} %get-tuple-element.28), channel_id=1, source_target_pairs={{0,2},{1,3},{2,0},{3,1},{4,6},{5,7},{6,4},{7,5},{8,10},{9,11},{10,... | collective-permute-start | bytes 589832 | tf_op jit(solution)/shard_map/ppermute | solution.py:16
  85.0 10.6 %collective-permute-start.25 = (f32[384,128]{1,0:T(8,128)S(1)}, f32[384,128]{1,0:T(8,128)S(1)}, u32[]{:S(2)}, u32[]{:S(2)}) collective-permute-start(f32[384,128]{1,0:T(8,128)S(1)} %add.55), channel_id=1, source_target_pairs={{0,6},{1,7},{2,4},{3,5},{4,2},{5,3},{6,0},{7,1},{8,14},{9,15},{10,... | collective-permute-start | bytes 589832 | tf_op jit(solution)/shard_map/ppermute | solution.py:16
  96.0 11.5 %collective-permute-start.26 = (f32[384,128]{1,0:T(8,128)S(1)}, f32[384,128]{1,0:T(8,128)S(1)}, u32[]{:S(2)}, u32[]{:S(2)}) collective-permute-start(f32[384,128]{1,0:T(8,128)S(1)} %fusion.53), channel_id=1, source_target_pairs={{0,14},{1,15},{2,12},{3,13},{4,10},{5,11},{6,8},{7,9},{8,22},{9,23... | collective-permute-start | bytes 589832 | tf_op jit(solution)/shard_map/ppermute | solution.py:27
  100.2 10.6 %collective-permute-start.30 = (f32[384,128]{1,0:T(8,128)S(1)}, f32[384,128]{1,0:T(8,128)S(1)}, u32[]{:S(2)}, u32[]{:S(2)}) collective-permute-start(f32[384,128]{1,0:T(8,128)S(1)} %fusion.53), channel_id=1, source_target_pairs={{0,10},{1,11},{2,8},{3,9},{4,14},{5,15},{6,12},{7,13},{8,18},{9,19... | collective-permute-start | bytes 589832 | tf_op jit(solution)/shard_map/ppermute | solution.py:27
  104.3 10.2 %collective-permute-start.27 = (f32[384,128]{1,0:T(8,128)S(1)}, f32[384,128]{1,0:T(8,128)S(1)}, u32[]{:S(2)}, u32[]{:S(2)}) collective-permute-start(f32[384,128]{1,0:T(8,128)S(1)} %fusion.53), channel_id=1, source_target_pairs={{0,8},{1,9},{2,10},{3,11},{4,12},{5,13},{6,14},{7,15},{8,16},{9,17... | collective-permute-start | bytes 589832 | tf_op jit(solution)/shard_map/ppermute | solution.py:27
  107.5 7.4 %collective-permute-start.32 = (f32[384,128]{1,0:T(8,128)S(1)}, f32[384,128]{1,0:T(8,128)S(1)}, u32[]{:S(2)}, u32[]{:S(2)}) collective-permute-start(f32[384,128]{1,0:T(8,128)S(1)} %collective-permute-done.26.refs_2_), channel_id=1, source_target_pairs={{0,2},{1,3},{2,0},{3,1},{4,6},{5,7},{6,4},{7,5},{8,10},{9,11},{10,... | collective-permute-start | bytes 589832 | tf_op jit(solution)/shard_map/ppermute | solution.py:16
  121.8 10.9 %collective-permute-start.35 = (f32[512,128]{1,0:T(8,128)S(1)}, f32[512,128]{1,0:T(8,128)S(1)}, u32[]{:S(2)}, u32[]{:S(2)}) collective-permute-start(f32[512,128]{1,0:T(8,128)S(1)} %slice.62), channel_id=1, source_target_pairs={{0,8},{8,16},{16,24},{1,9},{9,17},{17,25},{2,10},{10,18},{18,26},{... | collective-permute-start | bytes 786440 | tf_op jit(solution)/shard_map/ppermute | solution.py:301
  123.6 7.9 %collective-permute-start.37 = (f32[384,128]{1,0:T(8,128)S(1)}, f32[384,128]{1,0:T(8,128)S(1)}, u32[]{:S(2)}, u32[]{:S(2)}) collective-permute-start(f32[384,128]{1,0:T(8,128)S(1)} %parent_rows.10), channel_id=1, source_target_pairs={{0,2},{1,3},{2,0},{3,1},{4,6},{5,7},{6,4},{7,5},{8,10},{9,11},{10,... | collective-permute-start | bytes 589832 | tf_op jit(solution)/shard_map/ppermute | solution.py:16
  125.6 9.3 %collective-permute-start.36 = (f32[384,128]{1,0:T(8,128)S(1)}, f32[384,128]{1,0:T(8,128)S(1)}, u32[]{:S(2)}, u32[]{:S(2)}) collective-permute-start(f32[384,128]{1,0:T(8,128)S(1)} %get-tuple-element.34), channel_id=1, source_target_pairs={{0,2},{1,3},{2,0},{3,1},{4,6},{5,7},{6,4},{7,5},{8,10},{9,11},{10,... | collective-permute-start | bytes 589832 | tf_op jit(solution)/shard_map/ppermute | solution.py:16
  131.4 8.1 %collective-permute-start.38 = (f32[384,128]{1,0:T(8,128)S(1)}, f32[384,128]{1,0:T(8,128)S(1)}, u32[]{:S(2)}, u32[]{:S(2)}) collective-permute-start(f32[384,128]{1,0:T(8,128)S(1)} %add.60), channel_id=1, source_target_pairs={{0,6},{1,7},{2,4},{3,5},{4,2},{5,3},{6,0},{7,1},{8,14},{9,15},{10,... | collective-permute-start | bytes 589832 | tf_op jit(solution)/shard_map/ppermute | solution.py:16
  (27 other events, 107.9 us)

commit v4 on v3

--- a/solution.py
+++ b/solution.py
@@ -198,38 +198,6 @@
         name="parent_rows",
     )(place, parents, counts, rows, own, other)
     return dict(zip(wanted, found))
-
-
-def split_product(matrix, wide, columns):
-    high = matrix.astype(jnp.bfloat16)
-    low = (matrix - high.astype(jnp.float32)).astype(jnp.bfloat16)
-    return summed(jnp.dot(high, wide, preferred_element_type=jnp.float32)) + jnp.dot(
-        low, wide[:, :columns], preferred_element_type=jnp.float32
-    )
-
-
-def last_kernel(tick, downward, partial_solution, descended, earlier, out, result, sent):
-    del earlier
-    columns = result.shape[1]
-    result[...] = partial_solution[...] - split_product(downward[...], side_by_side(descended[...]), columns)
-    copy = pltpu.make_async_copy(result, out.at[tick], sent)
-    copy.start()
-    copy.wait()
-
-
-def last_leaf(downward, partial_solution, descended, earlier, tick):
-    vmem = pl.BlockSpec(memory_space=pltpu.VMEM)
-    return pl.pallas_call(
-        functools.partial(last_kernel, tick),
-        out_shape=jax.ShapeDtypeStruct(earlier.shape, jnp.float32),
-        in_specs=[vmem] * 3 + [pl.BlockSpec(memory_space=pl.ANY)],
-        out_specs=pl.BlockSpec(memory_space=pl.ANY),
-        scratch_shapes=[pltpu.VMEM(partial_solution.shape, jnp.float32), pltpu.SemaphoreType.DMA],
-        input_output_aliases={3: 0},
-        compiler_params=pltpu.CompilerParams(vmem_limit_bytes=VMEM_BYTES),
-        cost_estimate=pl.CostEstimate(flops=1000, bytes_accessed=1000, transcendentals=0),
-        name="last_leaf",
-    )(downward, partial_solution, descended, earlier)
 
 
 def local(
@@ -259,6 +227,7 @@
     place = myself.astype(jnp.int32).reshape(1)
     masks = cube_masks(fronts)
     span = offsets(masks)
+
     def edge(value):
         return value[leaf_order - iface_rows :]
 
@@ -311,9 +280,9 @@
                     if offset ^ mask not in held:
                         held[offset ^ mask] = swapped(held[offset], mask)
             leaf_now = partial_solution - product(downward, after(descended, moved[masks[0]]))
-            leaf_out = lax.dynamic_update_index_in_dim(leaf_out, leaf_now, tick, 0)
         else:
-            leaf_out = last_leaf(downward, partial_solution, descended, leaf_out, tick)
+            leaf_now = partial_solution - product(downward, descended)
+        leaf_out = lax.dynamic_update_index_in_dim(leaf_out, leaf_now, tick, 0)
         parent_out = lax.dynamic_update_index_in_dim(parent_out, solved, tick, 0)
     return (leaf_out[None, None], parent_out[None, None])
 

time: 143 us -> 144 us (level)
  Pallas kernels: 16 us -> 10.3 us
  starting transfers between devices: 48.4 us -> 53 us
    ppermute x29, starting transfers between devices: 25.4 us -> 31.5 us  [swapped(): lax.ppermute(value, 'front', [(place, place ^ mask) for place in range(co...]
    ppermute x29, waiting for transfers between devices: 34.2 us -> 31.1 us  [swapped(): lax.ppermute(value, 'front', [(place, place ^ mask) for place in range(co...]
    ppermute x8, waiting for transfers between devices: 14.4 us -> 17.2 us  [onward(): return lax.ppermute(value, ('panel', 'front'), pairs)]
    ppermute x8, starting transfers between devices: 20 us -> 17.4 us  [onward(): return lax.ppermute(value, ('panel', 'front'), pairs)]
    pallas_call x6, Pallas kernels: 6.6 us -> 4.26 us  [parent_rows(): pl.pallas_call(functools.partial(rows_kernel, wanted), out_shape=[jax.Sha...]
    pallas_call x3, Pallas kernels: 6.26 us -> 4.11 us  [parent_solve(): pl.pallas_call(functools.partial(solve_kernel, list(blocks)), out_shape=j...]
    dot_general x17 -> x18, matrix products: 22.5 us -> 23.1 us  [product(): jnp.dot(matrix, operand, precision=lax.Precision.HIGH, preferred_element_...]
  transfers between devices with their start and end apart: 39 -> 39, of which waited for: 22 -> 20; matrix products, arithmetic and copies ran while one was open for 15% -> 15% of each run, Pallas kernels for 6% -> 4%
where the time goes in v4:
time: 144 us; the launch traced here: 141 us
  starting transfers between devices  53 us (37%)
  waiting for transfers between devices  48.4 us (34%)
  matrix products  23.1 us (16%)
  Pallas kernels  10.3 us (7%)
  local copies, waits for them, and re-layouts  3.02 us (2%)
  other arithmetic  2.13 us (1%)
    ppermute x29, starting transfers between devices, swapped(): lax.ppermute(value, 'front', [(place, place ^ mask) for place in range(co...  31.5 us
    ppermute x29, waiting for transfers between devices, swapped(): lax.ppermute(value, 'front', [(place, place ^ mask) for place in range(co...  31.1 us
    dot_general x18, matrix products, product(): jnp.dot(matrix, operand, precision=lax.Precision.HIGH, preferred_element_...  23.1 us
    ppermute x8, starting transfers between devices, onward(): return lax.ppermute(value, ('panel', 'front'), pairs)  17.4 us
    ppermute x8, waiting for transfers between devices, onward(): return lax.ppermute(value, ('panel', 'front'), pairs)  17.2 us
    pallas_call x6, Pallas kernels, parent_rows(): pl.pallas_call(functools.partial(rows_kernel, wanted), out_shape=[jax.Sha...  4.26 us
    ppermute x2, starting transfers between devices, local(): lax.ppermute(leaving, 'panel', [(spot, spot + 1) for spot in range(panels...  4.12 us
    pallas_call x3, Pallas kernels, parent_solve(): pl.pallas_call(functools.partial(solve_kernel, list(blocks)), out_shape=j...  4.11 us
  transfers between devices with their start and end apart: 39, of which 20 were waited for; matrix products, arithmetic and copies ran while one was open for 15% of the time, Pallas kernels for 4%

profile of v4, /device:TPU:0, one launch (start us, length us, event | category | flops | bytes accessed | tf_op | source)
XLA Modules:
  0.0 141.1 jit_solution(17974573460214747086)
XLA Ops:
  5.0 3.1 %collective-permute-start.3 = (f32[384,128]{1,0:T(8,128)S(1)}, f32[384,128]{1,0:T(8,128)S(1)}, u32[]{:S(2)}, u32[]{:S(2)}) collective-permute-start(f32[384,128]{1,0:T(8,128)S(1)} %fusion.46.refs_0_), channel_id=1, source_target_pairs={{0,2},{1,3},{2,0},{3,1},{4,6},{5,7},{6,4},{7,5},{8,10},{9,11},{10,... | collective-permute-start | bytes 589832 | tf_op jit(solution)/shard_map/ppermute | solution.py:16
  8.1 2.5 %collective-permute-start.1 = (f32[384,128]{1,0:T(8,128)S(1)}, f32[384,128]{1,0:T(8,128)S(1)}, u32[]{:S(2)}, u32[]{:S(2)}) collective-permute-start(f32[384,128]{1,0:T(8,128)S(1)} %fusion.46.refs_0_), channel_id=1, source_target_pairs={{0,6},{1,7},{2,4},{3,5},{4,2},{5,3},{6,0},{7,1},{8,14},{9,15},{10,... | collective-permute-start | bytes 589832 | tf_op jit(solution)/shard_map/ppermute | solution.py:16
  10.6 2.8 %fusion.5 = f32[384,768]{1,0:T(8,128)} fusion(f32[1,1,768,768]{3,2,1,0:T(8,128)S(1)} %copy-done, f32[1,1,384,768]{3,2,1,0:T(8,128)S(1)} %copy-done.8), kind=kOutput, calls=%fused_computation.7 | convolution fusion | flops 1358954496 | bytes 4718592 | tf_op jit(solution)/shard_map/dot_general | solution.py:64
  13.4 3.8 %fusion.20 = f32[384,512]{1,0:T(8,128)} fusion(f32[384,768]{1,0:T(8,128)} %fusion.5, f32[1,1,768,512]{3,2,1,0:T(8,128)} %param.14, pred[]{:T(512)S(6)} %gt.3), kind=kOutput, calls=%fused_computation.20 | convolution fusion | flops 906166272 | bytes 3538945 | tf_op jit(solution)/shard_map/dot_general | solution.py:64
  17.2 2.4 %collective-permute-start.12 = (f32[384,512]{1,0:T(8,128)}, f32[384,512]{1,0:T(8,128)}, u32[]{:S(2)}, u32[]{:S(2)}) collective-permute-start(f32[384,512]{1,0:T(8,128)} %fusion.20), channel_id=1, source_target_pairs={{0,24},{1,25},{2,26},{3,27},{4,28},{5,29},{6,30},{7,31},{8,0},{9,1... | collective-permute-start | bytes 2359304 | tf_op jit(solution)/shard_map/ppermute | solution.py:27
  22.9 3.7 %collective-permute-done.5.refs_0_ = f32[384,128]{1,0:T(8,128)S(1)} collective-permute-done((f32[384,128]{1,0:T(8,128)S(1)}, f32[384,128]{1,0:T(8,128)S(1)}, u32[]{:S(2)}, u32[]{:S(2)}) %collective-permute-start.5) | collective-permute-done | bytes 196640 | tf_op jit(solution)/shard_map/ppermute | solution.py:16
  35.1 2.7 %collective-permute-done.12 = f32[384,512]{1,0:T(8,128)} collective-permute-done((f32[384,512]{1,0:T(8,128)}, f32[384,512]{1,0:T(8,128)}, u32[]{:S(2)}, u32[]{:S(2)}) %collective-permute-start.12) | collective-permute-done | bytes 786464 | tf_op jit(solution)/shard_map/ppermute | solution.py:27
  44.6 5.3 %collective-permute-done.10 = f32[384,128]{1,0:T(8,128)S(1)} collective-permute-done((f32[384,128]{1,0:T(8,128)S(1)}, f32[384,128]{1,0:T(8,128)S(1)}, u32[]{:S(2)}, u32[]{:S(2)}) %collective-permute-start.10) | collective-permute-done | bytes 196640 | tf_op jit(solution)/shard_map/ppermute | solution.py:16
  50.4 2.7 %collective-permute-start.13 = (f32[384,128]{1,0:T(8,128)S(1)}, f32[384,128]{1,0:T(8,128)S(1)}, u32[]{:S(2)}, u32[]{:S(2)}) collective-permute-start(f32[384,128]{1,0:T(8,128)S(1)} %fusion.60), channel_id=1, source_target_pairs={{0,14},{1,15},{2,12},{3,13},{4,10},{5,11},{6,8},{7,9},{8,22},{9,23... | collective-permute-start | bytes 589832 | tf_op jit(solution)/shard_map/ppermute | solution.py:27
  54.8 2.4 %collective-permute-start.14 = (f32[384,128]{1,0:T(8,128)S(1)}, f32[384,128]{1,0:T(8,128)S(1)}, u32[]{:S(2)}, u32[]{:S(2)}) collective-permute-start(f32[384,128]{1,0:T(8,128)S(1)} %fusion.60), channel_id=1, source_target_pairs={{0,8},{1,9},{2,10},{3,11},{4,12},{5,13},{6,14},{7,15},{8,16},{9,17... | collective-permute-start | bytes 589832 | tf_op jit(solution)/shard_map/ppermute | solution.py:27
  57.2 4.7 %collective-permute-done.13.refs_2_ = f32[384,128]{1,0:T(8,128)S(1)} collective-permute-done((f32[384,128]{1,0:T(8,128)S(1)}, f32[384,128]{1,0:T(8,128)S(1)}, u32[]{:S(2)}, u32[]{:S(2)}) %collective-permute-start.13) | collective-permute-done | bytes 196640 | tf_op jit(solution)/shard_map/ppermute | solution.py:27
  61.9 3.6 %collective-permute-start.19 = (f32[384,128]{1,0:T(8,128)S(1)}, f32[384,128]{1,0:T(8,128)S(1)}, u32[]{:S(2)}, u32[]{:S(2)}) collective-permute-start(f32[384,128]{1,0:T(8,128)S(1)} %collective-permute-done.13.refs_2_), channel_id=1, source_target_pairs={{0,2},{1,3},{2,0},{3,1},{4,6},{5,7},{6,4},{7,5},{8,10},{9,11},{10,... | collective-permute-start | bytes 589832 | tf_op jit(solution)/shard_map/ppermute | solution.py:16
  65.5 3.1 %collective-permute-done.14.refs_0_ = f32[384,128]{1,0:T(8,128)S(1)} collective-permute-done((f32[384,128]{1,0:T(8,128)S(1)}, f32[384,128]{1,0:T(8,128)S(1)}, u32[]{:S(2)}, u32[]{:S(2)}) %collective-permute-start.14) | collective-permute-done | bytes 196640 | tf_op jit(solution)/shard_map/ppermute | solution.py:27
  76.4 2.9 %collective-permute-start.24 = (f32[384,128]{1,0:T(8,128)S(1)}, f32[384,128]{1,0:T(8,128)S(1)}, u32[]{:S(2)}, u32[]{:S(2)}) collective-permute-start(f32[384,128]{1,0:T(8,128)S(1)} %parent_rows.8), channel_id=1, source_target_pairs={{0,2},{1,3},{2,0},{3,1},{4,6},{5,7},{6,4},{7,5},{8,10},{9,11},{10,... | collective-permute-start | bytes 589832 | tf_op jit(solution)/shard_map/ppermute | solution.py:16
  80.1 5.0 %collective-permute-done.24 = f32[384,128]{1,0:T(8,128)S(1)} collective-permute-done((f32[384,128]{1,0:T(8,128)S(1)}, f32[384,128]{1,0:T(8,128)S(1)}, u32[]{:S(2)}, u32[]{:S(2)}) %collective-permute-start.24) | collective-permute-done | bytes 196640 | tf_op jit(solution)/shard_map/ppermute | solution.py:16
  85.1 3.8 %collective-permute-start.25 = (f32[384,128]{1,0:T(8,128)S(1)}, f32[384,128]{1,0:T(8,128)S(1)}, u32[]{:S(2)}, u32[]{:S(2)}) collective-permute-start(f32[384,128]{1,0:T(8,128)S(1)} %add.56), channel_id=1, source_target_pairs={{0,6},{1,7},{2,4},{3,5},{4,2},{5,3},{6,0},{7,1},{8,14},{9,15},{10,... | collective-permute-start | bytes 589832 | tf_op jit(solution)/shard_map/ppermute | solution.py:16
  92.7 2.4 %collective-permute-done.25 = f32[384,128]{1,0:T(8,128)S(1)} collective-permute-done((f32[384,128]{1,0:T(8,128)S(1)}, f32[384,128]{1,0:T(8,128)S(1)}, u32[]{:S(2)}, u32[]{:S(2)}) %collective-permute-start.25) | collective-permute-done | bytes 196640 | tf_op jit(solution)/shard_map/ppermute | solution.py:16
  95.5 4.8 %collective-permute-start.26 = (f32[384,128]{1,0:T(8,128)S(1)}, f32[384,128]{1,0:T(8,128)S(1)}, u32[]{:S(2)}, u32[]{:S(2)}) collective-permute-start(f32[384,128]{1,0:T(8,128)S(1)} %fusion.59), channel_id=1, source_target_pairs={{0,14},{1,15},{2,12},{3,13},{4,10},{5,11},{6,8},{7,9},{8,22},{9,23... | collective-permute-start | bytes 589832 | tf_op jit(solution)/shard_map/ppermute | solution.py:27
  102.5 4.5 %collective-permute-done.26.refs_2_ = f32[384,128]{1,0:T(8,128)S(1)} collective-permute-done((f32[384,128]{1,0:T(8,128)S(1)}, f32[384,128]{1,0:T(8,128)S(1)}, u32[]{:S(2)}, u32[]{:S(2)}) %collective-permute-start.26) | collective-permute-done | bytes 196640 | tf_op jit(solution)/shard_map/ppermute | solution.py:27
  107.0 4.1 %collective-permute-start.32 = (f32[384,128]{1,0:T(8,128)S(1)}, f32[384,128]{1,0:T(8,128)S(1)}, u32[]{:S(2)}, u32[]{:S(2)}) collective-permute-start(f32[384,128]{1,0:T(8,128)S(1)} %collective-permute-done.26.refs_2_), channel_id=1, source_target_pairs={{0,2},{1,3},{2,0},{3,1},{4,6},{5,7},{6,4},{7,5},{8,10},{9,11},{10,... | collective-permute-start | bytes 589832 | tf_op jit(solution)/shard_map/ppermute | solution.py:16
  120.6 2.4 %collective-permute-start.35 = (f32[512,128]{1,0:T(8,128)S(1)}, f32[512,128]{1,0:T(8,128)S(1)}, u32[]{:S(2)}, u32[]{:S(2)}) collective-permute-start(f32[512,128]{1,0:T(8,128)S(1)} %slice.62), channel_id=1, source_target_pairs={{0,8},{8,16},{16,24},{1,9},{9,17},{17,25},{2,10},{10,18},{18,26},{... | collective-permute-start | bytes 786440 | tf_op jit(solution)/shard_map/ppermute | solution.py:270
  126.0 4.9 %collective-permute-done.37 = f32[384,128]{1,0:T(8,128)S(1)} collective-permute-done((f32[384,128]{1,0:T(8,128)S(1)}, f32[384,128]{1,0:T(8,128)S(1)}, u32[]{:S(2)}, u32[]{:S(2)}) %collective-permute-start.37) | collective-permute-done | bytes 196640 | tf_op jit(solution)/shard_map/ppermute | solution.py:16
  131.0 2.5 %collective-permute-start.38 = (f32[384,128]{1,0:T(8,128)S(1)}, f32[384,128]{1,0:T(8,128)S(1)}, u32[]{:S(2)}, u32[]{:S(2)}) collective-permute-start(f32[384,128]{1,0:T(8,128)S(1)} %add.61), channel_id=1, source_target_pairs={{0,6},{1,7},{2,4},{3,5},{4,2},{5,3},{6,0},{7,1},{8,14},{9,15},{10,... | collective-permute-start | bytes 589832 | tf_op jit(solution)/shard_map/ppermute | solution.py:16
  135.6 3.9 %collective-permute-done.38 = f32[384,128]{1,0:T(8,128)S(1)} collective-permute-done((f32[384,128]{1,0:T(8,128)S(1)}, f32[384,128]{1,0:T(8,128)S(1)}, u32[]{:S(2)}, u32[]{:S(2)}) %collective-permute-start.38) | collective-permute-done | bytes 196640 | tf_op jit(solution)/shard_map/ppermute | solution.py:16
  (121 shorter events, 56.1 us)
Async XLA Ops:
  5.0 17.4 %collective-permute-start.3 = (f32[384,128]{1,0:T(8,128)S(1)}, f32[384,128]{1,0:T(8,128)S(1)}, u32[]{:S(2)}, u32[]{:S(2)}) collective-permute-start(f32[384,128]{1,0:T(8,128)S(1)} %fusion.46.refs_0_), channel_id=1, source_target_pairs={{0,2},{1,3},{2,0},{3,1},{4,6},{5,7},{6,4},{7,5},{8,10},{9,11},{10,... | collective-permute-start | bytes 589832 | tf_op jit(solution)/shard_map/ppermute | solution.py:16
  8.1 11.5 %collective-permute-start.1 = (f32[384,128]{1,0:T(8,128)S(1)}, f32[384,128]{1,0:T(8,128)S(1)}, u32[]{:S(2)}, u32[]{:S(2)}) collective-permute-start(f32[384,128]{1,0:T(8,128)S(1)} %fusion.46.refs_0_), channel_id=1, source_target_pairs={{0,6},{1,7},{2,4},{3,5},{4,2},{5,3},{6,0},{7,1},{8,14},{9,15},{10,... | collective-permute-start | bytes 589832 | tf_op jit(solution)/shard_map/ppermute | solution.py:16
  10.6 16.1 %collective-permute-start = (f32[384,128]{1,0:T(8,128)S(1)}, f32[384,128]{1,0:T(8,128)S(1)}, u32[]{:S(2)}, u32[]{:S(2)}) collective-permute-start(f32[384,128]{1,0:T(8,128)S(1)} %fusion.46.refs_0_), channel_id=1, source_target_pairs={{0,1},{1,0},{2,3},{3,2},{4,5},{5,4},{6,7},{7,6},{8,9},{9,8},{10,11... | collective-permute-start | bytes 589832 | tf_op jit(solution)/shard_map/ppermute | solution.py:16
  17.2 20.7 %collective-permute-start.12 = (f32[384,512]{1,0:T(8,128)}, f32[384,512]{1,0:T(8,128)}, u32[]{:S(2)}, u32[]{:S(2)}) collective-permute-start(f32[384,512]{1,0:T(8,128)} %fusion.20), channel_id=1, source_target_pairs={{0,24},{1,25},{2,26},{3,27},{4,28},{5,29},{6,30},{7,31},{8,0},{9,1... | collective-permute-start | bytes 2359304 | tf_op jit(solution)/shard_map/ppermute | solution.py:27
  19.6 7.0 %collective-permute-start.5 = (f32[384,128]{1,0:T(8,128)S(1)}, f32[384,128]{1,0:T(8,128)S(1)}, u32[]{:S(2)}, u32[]{:S(2)}) collective-permute-start(f32[384,128]{1,0:T(8,128)S(1)} %collective-permute-done.1.refs_2_), channel_id=1, source_target_pairs={{0,2},{1,3},{2,0},{3,1},{4,6},{5,7},{6,4},{7,5},{8,10},{9,11},{10,... | collective-permute-start | bytes 589832 | tf_op jit(solution)/shard_map/ppermute | solution.py:16
  30.4 19.6 %collective-permute-start.11 = (f32[384,256]{1,0:T(8,128)S(1)}, f32[384,256]{1,0:T(8,128)S(1)}, u32[]{:S(2)}, u32[]{:S(2)}) collective-permute-start(f32[384,256]{1,0:T(8,128)S(1)} %fusion.52), channel_id=1, source_target_pairs={{0,24},{1,25},{2,26},{3,27},{4,28},{5,29},{6,30},{7,31},{8,0},{9,1... | collective-permute-start | bytes 1179656 | tf_op jit(solution)/shard_map/ppermute | solution.py:27
  33.3 7.5 %collective-permute-start.9 = (f32[384,128]{1,0:T(8,128)S(1)}, f32[384,128]{1,0:T(8,128)S(1)}, u32[]{:S(2)}, u32[]{:S(2)}) collective-permute-start(f32[384,128]{1,0:T(8,128)S(1)} %parent_rows.6), channel_id=1, source_target_pairs={{0,2},{1,3},{2,0},{3,1},{4,6},{5,7},{6,4},{7,5},{8,10},{9,11},{10,... | collective-permute-start | bytes 589832 | tf_op jit(solution)/shard_map/ppermute | solution.py:16
  40.8 9.1 %collective-permute-start.10 = (f32[384,128]{1,0:T(8,128)S(1)}, f32[384,128]{1,0:T(8,128)S(1)}, u32[]{:S(2)}, u32[]{:S(2)}) collective-permute-start(f32[384,128]{1,0:T(8,128)S(1)} %add.51), channel_id=1, source_target_pairs={{0,6},{1,7},{2,4},{3,5},{4,2},{5,3},{6,0},{7,1},{8,14},{9,15},{10,... | collective-permute-start | bytes 589832 | tf_op jit(solution)/shard_map/ppermute | solution.py:16
  50.4 11.5 %collective-permute-start.13 = (f32[384,128]{1,0:T(8,128)S(1)}, f32[384,128]{1,0:T(8,128)S(1)}, u32[]{:S(2)}, u32[]{:S(2)}) collective-permute-start(f32[384,128]{1,0:T(8,128)S(1)} %fusion.60), channel_id=1, source_target_pairs={{0,14},{1,15},{2,12},{3,13},{4,10},{5,11},{6,8},{7,9},{8,22},{9,23... | collective-permute-start | bytes 589832 | tf_op jit(solution)/shard_map/ppermute | solution.py:27
  53.1 12.4 %collective-permute-start.17 = (f32[384,128]{1,0:T(8,128)S(1)}, f32[384,128]{1,0:T(8,128)S(1)}, u32[]{:S(2)}, u32[]{:S(2)}) collective-permute-start(f32[384,128]{1,0:T(8,128)S(1)} %fusion.60), channel_id=1, source_target_pairs={{0,10},{1,11},{2,8},{3,9},{4,14},{5,15},{6,12},{7,13},{8,18},{9,19... | collective-permute-start | bytes 589832 | tf_op jit(solution)/shard_map/ppermute | solution.py:27
  54.8 13.7 %collective-permute-start.14 = (f32[384,128]{1,0:T(8,128)S(1)}, f32[384,128]{1,0:T(8,128)S(1)}, u32[]{:S(2)}, u32[]{:S(2)}) collective-permute-start(f32[384,128]{1,0:T(8,128)S(1)} %fusion.60), channel_id=1, source_target_pairs={{0,8},{1,9},{2,10},{3,11},{4,12},{5,13},{6,14},{7,15},{8,16},{9,17... | collective-permute-start | bytes 589832 | tf_op jit(solution)/shard_map/ppermute | solution.py:27
  61.9 7.2 %collective-permute-start.19 = (f32[384,128]{1,0:T(8,128)S(1)}, f32[384,128]{1,0:T(8,128)S(1)}, u32[]{:S(2)}, u32[]{:S(2)}) collective-permute-start(f32[384,128]{1,0:T(8,128)S(1)} %collective-permute-done.13.refs_2_), channel_id=1, source_target_pairs={{0,2},{1,3},{2,0},{3,1},{4,6},{5,7},{6,4},{7,5},{8,10},{9,11},{10,... | collective-permute-start | bytes 589832 | tf_op jit(solution)/shard_map/ppermute | solution.py:16
  74.7 14.2 %collective-permute-start.22 = (f32[512,128]{1,0:T(8,128)S(1)}, f32[512,128]{1,0:T(8,128)S(1)}, u32[]{:S(2)}, u32[]{:S(2)}) collective-permute-start(f32[512,128]{1,0:T(8,128)S(1)} %slice.58), channel_id=1, source_target_pairs={{0,8},{8,16},{16,24},{1,9},{9,17},{17,25},{2,10},{10,18},{18,26},{... | collective-permute-start | bytes 786440 | tf_op jit(solution)/shard_map/ppermute | solution.py:270
  76.4 8.6 %collective-permute-start.24 = (f32[384,128]{1,0:T(8,128)S(1)}, f32[384,128]{1,0:T(8,128)S(1)}, u32[]{:S(2)}, u32[]{:S(2)}) collective-permute-start(f32[384,128]{1,0:T(8,128)S(1)} %parent_rows.8), channel_id=1, source_target_pairs={{0,2},{1,3},{2,0},{3,1},{4,6},{5,7},{6,4},{7,5},{8,10},{9,11},{10,... | collective-permute-start | bytes 589832 | tf_op jit(solution)/shard_map/ppermute | solution.py:16
  80.0 12.6 %collective-permute-start.23 = (f32[384,128]{1,0:T(8,128)S(1)}, f32[384,128]{1,0:T(8,128)S(1)}, u32[]{:S(2)}, u32[]{:S(2)}) collective-permute-start(f32[384,128]{1,0:T(8,128)S(1)} %get-tuple-element.28), channel_id=1, source_target_pairs={{0,2},{1,3},{2,0},{3,1},{4,6},{5,7},{6,4},{7,5},{8,10},{9,11},{10,... | collective-permute-start | bytes 589832 | tf_op jit(solution)/shard_map/ppermute | solution.py:16
  85.1 9.9 %collective-permute-start.25 = (f32[384,128]{1,0:T(8,128)S(1)}, f32[384,128]{1,0:T(8,128)S(1)}, u32[]{:S(2)}, u32[]{:S(2)}) collective-permute-start(f32[384,128]{1,0:T(8,128)S(1)} %add.56), channel_id=1, source_target_pairs={{0,6},{1,7},{2,4},{3,5},{4,2},{5,3},{6,0},{7,1},{8,14},{9,15},{10,... | collective-permute-start | bytes 589832 | tf_op jit(solution)/shard_map/ppermute | solution.py:16
  95.5 11.5 %collective-permute-start.26 = (f32[384,128]{1,0:T(8,128)S(1)}, f32[384,128]{1,0:T(8,128)S(1)}, u32[]{:S(2)}, u32[]{:S(2)}) collective-permute-start(f32[384,128]{1,0:T(8,128)S(1)} %fusion.59), channel_id=1, source_target_pairs={{0,14},{1,15},{2,12},{3,13},{4,10},{5,11},{6,8},{7,9},{8,22},{9,23... | collective-permute-start | bytes 589832 | tf_op jit(solution)/shard_map/ppermute | solution.py:27
  100.2 10.9 %collective-permute-start.30 = (f32[384,128]{1,0:T(8,128)S(1)}, f32[384,128]{1,0:T(8,128)S(1)}, u32[]{:S(2)}, u32[]{:S(2)}) collective-permute-start(f32[384,128]{1,0:T(8,128)S(1)} %fusion.59), channel_id=1, source_target_pairs={{0,10},{1,11},{2,8},{3,9},{4,14},{5,15},{6,12},{7,13},{8,18},{9,19... | collective-permute-start | bytes 589832 | tf_op jit(solution)/shard_map/ppermute | solution.py:27
  102.5 10.9 %collective-permute-start.27 = (f32[384,128]{1,0:T(8,128)S(1)}, f32[384,128]{1,0:T(8,128)S(1)}, u32[]{:S(2)}, u32[]{:S(2)}) collective-permute-start(f32[384,128]{1,0:T(8,128)S(1)} %fusion.59), channel_id=1, source_target_pairs={{0,8},{1,9},{2,10},{3,11},{4,12},{5,13},{6,14},{7,15},{8,16},{9,17... | collective-permute-start | bytes 589832 | tf_op jit(solution)/shard_map/ppermute | solution.py:27
  107.0 8.3 %collective-permute-start.32 = (f32[384,128]{1,0:T(8,128)S(1)}, f32[384,128]{1,0:T(8,128)S(1)}, u32[]{:S(2)}, u32[]{:S(2)}) collective-permute-start(f32[384,128]{1,0:T(8,128)S(1)} %collective-permute-done.26.refs_2_), channel_id=1, source_target_pairs={{0,2},{1,3},{2,0},{3,1},{4,6},{5,7},{6,4},{7,5},{8,10},{9,11},{10,... | collective-permute-start | bytes 589832 | tf_op jit(solution)/shard_map/ppermute | solution.py:16
  120.6 12.9 %collective-permute-start.35 = (f32[512,128]{1,0:T(8,128)S(1)}, f32[512,128]{1,0:T(8,128)S(1)}, u32[]{:S(2)}, u32[]{:S(2)}) collective-permute-start(f32[512,128]{1,0:T(8,128)S(1)} %slice.62), channel_id=1, source_target_pairs={{0,8},{8,16},{16,24},{1,9},{9,17},{17,25},{2,10},{10,18},{18,26},{... | collective-permute-start | bytes 786440 | tf_op jit(solution)/shard_map/ppermute | solution.py:270
  123.0 7.9 %collective-permute-start.37 = (f32[384,128]{1,0:T(8,128)S(1)}, f32[384,128]{1,0:T(8,128)S(1)}, u32[]{:S(2)}, u32[]{:S(2)}) collective-permute-start(f32[384,128]{1,0:T(8,128)S(1)} %parent_rows.10), channel_id=1, source_target_pairs={{0,2},{1,3},{2,0},{3,1},{4,6},{5,7},{6,4},{7,5},{8,10},{9,11},{10,... | collective-permute-start | bytes 589832 | tf_op jit(solution)/shard_map/ppermute | solution.py:16
  125.9 9.6 %collective-permute-start.36 = (f32[384,128]{1,0:T(8,128)S(1)}, f32[384,128]{1,0:T(8,128)S(1)}, u32[]{:S(2)}, u32[]{:S(2)}) collective-permute-start(f32[384,128]{1,0:T(8,128)S(1)} %get-tuple-element.34), channel_id=1, source_target_pairs={{0,2},{1,3},{2,0},{3,1},{4,6},{5,7},{6,4},{7,5},{8,10},{9,11},{10,... | collective-permute-start | bytes 589832 | tf_op jit(solution)/shard_map/ppermute | solution.py:16
  131.0 8.5 %collective-permute-start.38 = (f32[384,128]{1,0:T(8,128)S(1)}, f32[384,128]{1,0:T(8,128)S(1)}, u32[]{:S(2)}, u32[]{:S(2)}) collective-permute-start(f32[384,128]{1,0:T(8,128)S(1)} %add.61), channel_id=1, source_target_pairs={{0,6},{1,7},{2,4},{3,5},{4,2},{5,3},{6,0},{7,1},{8,14},{9,15},{10,... | collective-permute-start | bytes 589832 | tf_op jit(solution)/shard_map/ppermute | solution.py:16
  (27 other events, 105.6 us)
